TPU v7x, 32 devices: a whole 2x2x4 slice. The times are simulated.
32 devices in a mesh: section: 2 (over core), dp: 4 (over z), ctx: 4 (over y, x).
Axes of the slice: x: 2, y: 2, z: 4, core: 2. Of those that a mesh axis runs over, the one named last changes fastest.
Arguments:
- ends: bfloat16 [2, 2, 3584, 960], P('section', None, ('dp', 'ctx')), may hold values from -6 to 6
- doc_lengths: int32 [2, 4, 2], P(None, 'dp'), may hold values from 0 to 896, as said below
- w_query: bfloat16 [960, 960], replicated, may hold values from -0.1875 to 0.1875
- key_projection_weight: bfloat16 [960, 320], replicated, may hold values from -0.1875 to 0.1875
- value_projection_weight: bfloat16 [960, 320], replicated, may hold values from -0.1875 to 0.1875
- w_out: bfloat16 [960, 960], replicated, may hold values from -0.75 to 0.75
- w_gate: bfloat16 [960, 2560], replicated, may hold values from -0.1875 to 0.1875
- w_up: bfloat16 [960, 2560], replicated, may hold values from -0.1875 to 0.1875
- w_down: bfloat16 [2560, 960], replicated, may hold values from -0.125 to 0.125
- gain_attn: bfloat16 [960], replicated, may hold values from 0.5 to 1.5
- gain_ffn: bfloat16 [960], replicated, may hold values from 0.5 to 1.5
Outputs:
- acts: bfloat16 [2, 2, 3584, 960], P('section', None, ('dp', 'ctx'))
- grads_in: bfloat16 [2, 2, 3584, 960], P('section', None, ('dp', 'ctx'))
- grad_w_query: float32 [960, 960], P('dp')
- grad_w_key: float32 [960, 320], P('dp')
- grad_w_value: float32 [960, 320], P('dp')
- grad_w_out: float32 [960, 960], P('dp')
- grad_w_gate: float32 [960, 2560], P('dp')
- grad_w_up: float32 [960, 2560], P('dp')
- grad_w_down: float32 [2560, 960], P('dp')
- grad_gain_attn: float32 [960], P('dp')
- grad_gain_ffn: float32 [960], P('dp')
Inputs may be any that keep to these rules, and one draw needn't show every extreme that they name: `doc_lengths`: each row holds either one sequence of 896 tokens followed by an empty slot, or a sequence of 512 tokens followed by one of 384. Of the two micro-batches' rows at the same index of dimension 1, exactly one holds the single sequence.
All inputs are finite; a program needn't handle non-finite values.
Results may differ from a plain program's by a relative error of at most 0.028.
Values may be sent and summed in bfloat16 or wider, within the bound.
A program may use at most 192 MiB of HBM per device.

v0:
```python
import jax
import jax.numpy as jnp
import numpy as np
from jax import lax
from jax.experimental import pallas as pl
from jax.experimental.pallas import tpu as pltpu
from jax.sharding import PartitionSpec as P

MESH = pl.DeviceIdType.MESH
QUERY_HEADS = 15
KEY_VALUE_HEADS = 5
HEAD_SIZE = 64
SHARE = QUERY_HEADS // KEY_VALUE_HEADS
RANKS = 4
epsilon = 1e-05
masked_fill = -1e30
F32 = jnp.float32
BF16 = jnp.bfloat16


def dot(left, right):
    return jnp.dot(left, right, preferred_element_type=F32)


def dot_rt(left, right):
    return lax.dot_general(left, right, (((1,), (1,)), ((), ())), preferred_element_type=F32)


def dot_lt(left, right):
    return lax.dot_general(left, right, (((0,), (0,)), ((), ())), preferred_element_type=F32)


def tiles(total, width):
    return [(at, min(width, total - at)) for at in range(0, total, width)]


def wide(block):
    missing = 128 - block.shape[1]
    if not missing:
        return block
    return jnp.concatenate([block, jnp.zeros((block.shape[0], missing), block.dtype)], axis=1)


def lanes(rows):
    return lax.broadcasted_iota(jnp.int32, (rows, 128), 1)


def half_turn(block):
    front = lanes(block.shape[0]) % HEAD_SIZE < HEAD_SIZE // 2
    return jnp.where(front, pltpu.roll(block, 96, 1), pltpu.roll(block, 32, 1))


def inverse_rms(hidden):
    return lax.rsqrt(jnp.mean(hidden * hidden, axis=-1, keepdims=True) + epsilon)


def half_turned(block, cosines, sines, direction):
    return block * cosines + direction * (half_turn(block) * sines)


def norm_back(hidden, gain, upstream):
    scale = inverse_rms(hidden)
    weighted = upstream * gain
    inside = jnp.mean(weighted * hidden, axis=-1, keepdims=True)
    gain_row = jnp.sum(upstream * hidden * scale, axis=0, keepdims=True)
    return scale * weighted - hidden * (scale * scale * scale * inside), gain_row


def start_if(condition, here, there):
    @pl.when(condition)
    def _():
        here().start()

    @pl.when(jnp.logical_not(condition))
    def _():
        there().start()


class AttentionBack:
    def __init__(
        self, rank, device_of, qd, kv, o_raw, allowed, cos_sin, ra, pds, dkv, dkv_in, gkv, send, recv
    ):
        self.rank, self.device_of = rank, device_of
        self.qd, self.kv, self.o_raw, self.allowed, self.cos_sin = qd, kv, o_raw, allowed, cos_sin
        self.ra, self.pds, self.dkv, self.dkv_in, self.gkv = ra, pds, dkv, dkv_in, gkv
        self.send_sem, self.recv_sem = send, recv
        self.rows, self.width = ra.shape[1:]

    def head(self, g):
        rows = self.rows
        kv_g = self.kv[g]
        for i in range(SHARE):
            mine = slice(i * rows, (i + 1) * rows)
            other = slice((SHARE + i) * rows, (SHARE + i + 1) * rows)
            kept = self.o_raw[g * SHARE + i]
            scores = dot_rt(self.qd[g, mine, :], kv_g) + self.allowed[...]
            probs = jnp.exp(scores - kept[:, 0:1])
            grad_out = self.qd[g, other, :]
            grad_probs = dot_rt(grad_out, kv_g)
            weight = jnp.sum(grad_out.astype(F32) * kept, axis=-1, keepdims=True)
            grad_scores = (probs * (grad_probs - weight)).astype(BF16)
            self.pds[mine, :] = grad_scores
            self.pds[other, :] = probs.astype(BF16)
            self.o_raw[g * SHARE + i] = dot(grad_scores, kv_g)
        grad_kv = dot_lt(self.qd[g], self.pds[...])
        self.dkv[g] = grad_kv.T.astype(BF16)
        self.send(g)

    def heads(self, first, last):
        def body(g, carry):
            self.head(g)

            @pl.when(g > 0)
            def _():
                self.relay(g - 1)

            return carry

        lax.fori_loop(first, last, body, 0)

    def copy(self, quarter, count, dst, slot_in, slot, g):
        rows = self.rows
        return pltpu.make_async_remote_copy(
            src_ref=self.dkv.at[g, pl.ds(quarter * rows, count * rows)],
            dst_ref=self.dkv_in.at[g, pl.ds(slot_in * rows, count * rows)],
            send_sem=self.send_sem.at[slot, g],
            recv_sem=self.recv_sem.at[slot_in, g],
            device_id=self.device_of(dst),
            device_id_type=MESH,
        )

    def add(self, quarter, slots, g):
        rows = self.rows
        span = slice(quarter * rows, (quarter + 1) * rows)
        total = self.dkv[g, span].astype(F32)
        for slot in slots:
            total = total + self.dkv_in[g, slot * rows : (slot + 1) * rows].astype(F32)
        self.dkv[g, span] = total.astype(BF16)

    def send(self, g):
        @pl.when(self.rank == 3)
        def _():
            self.copy(2, 1, 2, 0, 0, g).start()
            self.copy(0, 2, 1, 0, 1, g).start()

        @pl.when(self.rank == 2)
        def _():
            self.copy(1, 1, 1, 2, 0, g).start()
            self.copy(0, 1, 0, 1, 1, g).start()

    def relay(self, g):
        @pl.when(self.rank == 1)
        def _():
            self.copy(0, 2, 1, 0, 0, g).wait_recv()
            self.add(0, (0,), g)
            self.copy(0, 1, 0, 0, 0, g).start()

    def queries(self):
        for at, size in tiles(self.width, 128):
            head = at // HEAD_SIZE
            block = self.o_raw[head]
            if size == 128:
                low = lanes(self.rows) < HEAD_SIZE
                block = jnp.where(low, block, pltpu.roll(self.o_raw[head + 1], 64, 1))
            turned = half_turned(block, self.cos_sin[0], self.cos_sin[1], -1.0) * 0.125
            self.ra[0, :, at : at + size] = turned[:, :size].astype(BF16)

    def collect(self):
        low = lanes(self.rows) < HEAD_SIZE
        cosines = jnp.where(low, self.cos_sin[0], 1.0)
        sines = jnp.where(low, self.cos_sin[1], 0.0)
        mine = pl.ds(pl.multiple_of(self.rank * self.rows, 16), self.rows)
        for g in range(KEY_VALUE_HEADS):
            self.arrive(g)
            block = half_turned(self.dkv[g, mine, :].astype(F32), cosines, sines, -1.0)
            self.gkv[:, 128 * g : 128 * g + 128] = block.astype(BF16)

    def arrive(self, g):
        @pl.when(self.rank == 3)
        def _():
            self.copy(2, 1, 2, 0, 0, g).wait_send()
            self.copy(0, 2, 1, 0, 1, g).wait_send()

        @pl.when(self.rank == 2)
        def _():
            self.copy(0, 1, 2, 0, 0, g).wait_recv()
            self.copy(1, 1, 1, 2, 0, g).wait_send()
            self.copy(0, 1, 0, 1, 1, g).wait_send()
            self.add(2, (0,), g)

        @pl.when(self.rank == 1)
        def _():
            self.copy(0, 1, 2, 2, 0, g).wait_recv()
            self.copy(0, 1, 0, 0, 0, g).wait_send()
            self.add(1, (1, 2), g)

        @pl.when(self.rank == 0)
        def _():
            self.copy(0, 1, 2, 0, 0, g).wait_recv()
            self.copy(0, 1, 2, 1, 0, g).wait_recv()
            self.add(0, (0, 1), g)

    def project(self, total, wq, wkv):
        for at, size in tiles(self.width, 256):
            total[:, at : at + size] = dot_rt(self.ra[0], wq[at : at + size, :]) + dot(
                self.gkv[...], wkv[:, at : at + size]
            )


class OutCopy:
    def __init__(self, out, send, recv):
        self.section, self.dp, ctx = (lax.axis_index(a) for a in ("section", "dp", "ctx"))
        self.home = 2 * self.section + ctx % 2
        self.ctx, self.micro = ctx, ctx // 2
        self.out, self.send, self.recv = out, send, recv

    def here(self, l):
        return (self.section == l) & (self.ctx == self.home)

    def remote(self, array, l):
        return pltpu.make_async_remote_copy(
            src_ref=array,
            dst_ref=self.out.at[0, self.micro],
            send_sem=self.send.at[l],
            recv_sem=self.recv.at[self.micro],
            device_id=(l, self.dp, self.home),
            device_id_type=MESH,
        )

    def local(self, array):
        return pltpu.make_async_copy(array, self.out.at[0, self.micro], self.recv.at[self.micro])

    def start(self, array, l):
        start_if(self.here(l), lambda: self.local(array), lambda: self.remote(array, l))

    def sent(self, array, l):
        @pl.when(jnp.logical_not(self.here(l)))
        def _():
            self.remote(array, l).wait_send()

    def arrived(self, array):
        for block in range(2):
            pltpu.make_async_copy(array, self.out.at[0, block], self.recv.at[block]).wait()


def greet(barrier, dp):
    section, ctx = lax.axis_index("section"), lax.axis_index("ctx")
    for step in range(1, 8):
        other = (4 * section + ctx + step) % 8
        pl.semaphore_signal(
            barrier, inc=1, device_id=(other // 4, dp, other % 4), device_id_type=MESH
        )


def layers_kernel(complete, *refs):
    refs = list(refs)

    def take(count):
        taken = refs[:count]
        del refs[:count]
        return taken

    lengths, ends, frequency, gain_a, gain_f, wq_h, wk_h, wv_h, wo_h, wg_h, wu_h, wd_h = take(12)
    acts_o, grads_o, gain_o, nf_o, in_o, gg_o, gu_o, br_o, la_o, ra_o, nr_o, kvg_o = take(12)
    kept_o = [] if complete else take(7)
    wq, wkv, wo, wg, wu, wd = take(6)
    act, go, middle, norm_ffn, fact_a, fact_b, inner, lm, qd, kv, o_raw = take(11)
    sum_acc, gm, gg, gu, br, ra, pds, dkv, dkv_in, gkv, cos_sin, allowed_add, gain_v = take(13)
    w_sem, kv_sem, in_send, in_recv, kv_send, kv_recv, dk_send, dk_recv = take(8)
    act_send, act_recv, grad_send, grad_recv, op_own, op_send, op_recv, kept_sem = take(8)

    section = lax.axis_index("section")
    dp = lax.axis_index("dp")
    ctx = lax.axis_index("ctx")
    micro = ctx // 2
    xbit = ctx % 2
    rank = 2 * section + xbit
    rows, width = act.shape[1], act.shape[2]
    ff = wg.shape[1]
    ff_half = ff // 2

    def device_of(r):
        return (r // 2, dp, 2 * micro + r % 2)

    partner = (1 - section, dp, ctx)

    loads = [
        pltpu.make_async_copy(h, v, w_sem.at[i])
        for i, (h, v) in enumerate([(wq_h, wq), (wo_h, wo), (wg_h, wg), (wu_h, wu), (wd_h, wd)])
    ]
    kv_loads = [
        pltpu.make_async_copy(
            h.at[pl.ds(g * HEAD_SIZE, HEAD_SIZE)],
            wkv.at[pl.ds((2 * g + i) * HEAD_SIZE, HEAD_SIZE)],
            kv_sem.at[i, g],
        )
        for g in range(KEY_VALUE_HEADS)
        for i, h in enumerate((wk_h, wv_h))
    ]
    for load in kv_loads + loads:
        load.start()
    kv[...] = jnp.zeros_like(kv)
    barrier = pltpu.get_barrier_semaphore()
    greet(barrier, dp)
    pl.semaphore_wait(barrier, 7)

    def in_local(block, into_x):
        dst, slot = (act.at[0], 0) if into_x else (go.at[2], 1)
        return pltpu.make_async_copy(ends.at[0, block], dst, in_recv.at[slot])

    def in_remote(block, into_x):
        dst, slot = (act.at[0], 0) if into_x else (go.at[2], 1)
        return pltpu.make_async_remote_copy(
            src_ref=ends.at[0, block],
            dst_ref=dst,
            send_sem=in_send.at[block],
            recv_sem=in_recv.at[slot],
            device_id=(ctx // 2, dp, 2 * block + xbit),
            device_id_type=MESH,
        )

    def in_mine(block):
        return (section == ctx // 2) & (ctx // 2 == block)

    def in_start(into_x):
        @pl.when(section == (0 if into_x else 1))
        def _():
            for block in range(2):
                start_if(
                    in_mine(block),
                    lambda block=block: in_local(block, into_x),
                    lambda block=block: in_remote(block, into_x),
                )

    in_start(True)
    lane = lanes(rows)
    low = lane < HEAD_SIZE
    gain_attn = gain_a[...].astype(F32).reshape(1, width)
    gain_ffn = gain_f[...].astype(F32).reshape(1, width)

    def place(token_index):
        segment = jnp.zeros_like(token_index)
        start = jnp.zeros_like(token_index)
        finish = jnp.int32(0)
        for slot in range(lengths.shape[2]):
            length = lengths[micro, 0, slot]
            finish = finish + length
            passed = (token_index >= finish).astype(jnp.int32)
            segment = segment + passed
            start = start + passed * length
        return segment, token_index - start

    seg_mine, position = place(rank * rows + lax.broadcasted_iota(jnp.int32, (rows, 128), 0))
    angles = position.astype(F32) * frequency[...]
    cos_sin[0] = jnp.cos(angles)
    cos_sin[1] = jnp.where(lane % HEAD_SIZE < HEAD_SIZE // 2, -1.0, 1.0) * jnp.sin(angles)
    key_index = lax.broadcasted_iota(jnp.int32, (1, RANKS * rows), 1)
    query_index = rank * rows + lax.broadcasted_iota(jnp.int32, (rows, 1), 0)
    allowed_add[...] = jnp.where(
        (seg_mine[:, 0:1] == place(key_index)[0]) & (query_index >= key_index), 0.0, masked_fill
    )

    def kv_rows(l, r, g):
        return kv.at[l, g, pl.ds(r * rows, rows)]

    def kv_copy(l, quarter, dst, slot, g):
        return pltpu.make_async_remote_copy(
            src_ref=kv_rows(l, quarter, g),
            dst_ref=kv_rows(l, quarter, g),
            send_sem=kv_send.at[l, slot, g],
            recv_sem=kv_recv.at[l, quarter, g],
            device_id=device_of(dst),
            device_id_type=MESH,
        )

    kv_plan = [(0, 0, 1, 0), (0, 0, 2, 1), (1, 1, 2, 0), (1, 1, 3, 1), (2, 2, 3, 0)]
    kv_relay = (1, 0, 3, 2)

    def kv_start(l, g):
        for sender, quarter, dst, slot in kv_plan:

            @pl.when(rank == sender)
            def _(quarter=quarter, dst=dst, slot=slot):
                kv_copy(l, quarter, dst, slot, g).start()

    def kv_relayed(l, g):
        @pl.when(rank == 1)
        def _():
            kv_copy(l, 0, 3, 2, g).wait_recv()
            kv_copy(l, 0, 3, 2, g).start()

    def kv_finish(l, g):

        for quarter, receivers in ((0, (2, 3)), (1, (2, 3)), (2, (3,))):
            for receiver in receivers:

                @pl.when(rank == receiver)
                def _(quarter=quarter):
                    kv_copy(l, quarter, 0, 0, g).wait_recv()

    def kv_sent(l):
        for sender, quarter, dst, slot in kv_plan + [kv_relay]:

            @pl.when(rank == sender)
            def _(quarter=quarter, dst=dst, slot=slot):
                for g in range(KEY_VALUE_HEADS):
                    kv_copy(l, quarter, dst, slot, g).wait_send()

    acts_out = OutCopy(acts_o, act_send, act_recv)
    grads_out = OutCopy(grads_o, grad_send, grad_recv)

    def op_copy(kind, l, own):
        role = section if own else 1 - section
        half = pl.ds(pl.multiple_of(role * ff_half, 128), ff_half)
        src = [
            lambda: norm_ffn.at[l],
            lambda: inner.at[l],
            lambda: gg.at[:, half],
            lambda: gu.at[:, half],
            lambda: br.at[:, pl.ds(pl.multiple_of(role * 512, 128), 512)],
            lambda: lm.at[l, role],
            lambda: ra.at[role],
            lambda: lm.at[l, 0],
            lambda: gkv.at[:, pl.ds(pl.multiple_of(role * 256, 128), 384)],
        ][kind]()
        block = section if kind in (6, 8) and not complete else 2 * section + l
        dst = [nf_o, in_o, gg_o, gu_o, br_o, la_o, ra_o, nr_o, kvg_o][kind].at[
            pl.ds(pl.multiple_of(block * rows, 16), rows)
        ]
        if own:
            return pltpu.make_async_copy(src, dst, op_own.at[kind, l])
        return pltpu.make_async_remote_copy(
            src_ref=src,
            dst_ref=dst,
            send_sem=op_send.at[kind, l],
            recv_sem=op_recv.at[kind, l],
            device_id=partner,
            device_id_type=MESH,
        )

    def op_start(kinds, l):
        for kind in kinds:
            op_copy(kind, l, True).start()
            op_copy(kind, l, False).start()

    def op_sent(kinds, l):
        for kind in kinds:
            op_copy(kind, l, True).wait()
            op_copy(kind, l, False).wait_send()

    def kept_copy(i):
        src = [act.at[0], kv.at[0], o_raw.at[0], cos_sin, allowed_add, qd.at[0], gm][i]
        return pltpu.make_async_copy(src, kept_o[i], kept_sem.at[i])

    def kept_start(*which):
        if not complete:
            for i in which:
                kept_copy(i).start()

    in_remote(0, True).wait_recv()
    for load in kv_loads:
        load.wait()

    def forward(l, carry):
        hidden = act[l].astype(F32)
        cos_q, sin_q = cos_sin[0], cos_sin[1]
        lm[l, 0] = (hidden * inverse_rms(hidden) * gain_attn).astype(BF16)
        cos_kv = jnp.where(low, cos_q, 1.0)
        sin_kv = jnp.where(low, sin_q, 0.0)
        mine = pl.ds(pl.multiple_of(rank * rows, 16), rows)
        for g in range(KEY_VALUE_HEADS):
            block = dot_rt(lm[l, 0], wkv[128 * g : 128 * g + 128, :])
            turned = half_turned(block, cos_kv, sin_kv, 1.0)
            kv[l, g, mine, :] = turned.astype(BF16)
            kv_start(l, g)

        @pl.when(l == 0)
        def _():
            loads[0].wait()
            in_start(False)
            kept_start(0, 3, 4)

        for at, size in tiles(width, 256):
            product = dot(lm[l, 0], wq[:, at : at + size])
            for inside, part in tiles(size, 128):
                block = wide(product[:, inside : inside + part])
                turned = half_turned(block, cos_q, sin_q, 1.0) * 0.125
                head = (at + inside) // HEAD_SIZE
                qd[l, head // SHARE, pl.ds(head % SHARE * rows, rows), :] = jnp.where(
                    low, turned, 0.0
                ).astype(BF16)
                head += 1
                if head < QUERY_HEADS:
                    qd[l, head // SHARE, pl.ds(head % SHARE * rows, rows), :] = jnp.where(
                        low, pltpu.roll(turned, 64, 1), 0.0
                    ).astype(BF16)
        kv_relayed(l, 0)
        kv_finish(l, 0)

        def heads(g, carry):
            @pl.when(g < KEY_VALUE_HEADS - 1)
            def _():
                kv_relayed(l, g + 1)

            @pl.when(g > 0)
            def _():
                kv_finish(l, g)

            kv_g = kv[l, g]
            for i in range(SHARE):
                scores = dot_rt(qd[l, g, i * rows : (i + 1) * rows, :], kv_g) + allowed_add[...]
                peak = jnp.max(scores, axis=-1, keepdims=True)
                exponent = jnp.exp(scores - peak)
                total = jnp.sum(exponent, axis=-1, keepdims=True)
                out = dot(exponent.astype(BF16), kv_g) * (1.0 / total)
                o_raw[l, g * SHARE + i] = jnp.where(low, peak + jnp.log(total), out)
            return carry

        lax.fori_loop(0, KEY_VALUE_HEADS, heads, 0)

        @pl.when(l == 0)
        def _():
            kept_start(1, 2)
            loads[1].wait()

        for at, size in tiles(width, 128):
            head = at // HEAD_SIZE
            block = pltpu.roll(o_raw[l, head], 64, 1)
            if size == 128:
                block = jnp.where(low, block, o_raw[l, head + 1])
            lm[l, 1, :, at : at + size] = block[:, :size].astype(BF16)
        for at, size in tiles(width, 256):
            middle[l, :, at : at + size] = act[l, :, at : at + size].astype(F32) + dot(
                lm[l, 1], wo[:, at : at + size]
            )
        mid = middle[l]
        norm_ffn[l] = (mid * inverse_rms(mid) * gain_ffn).astype(BF16)
        op_start((0, 5, 7), l)

        @pl.when(l == 0)
        def _():
            loads[2].wait()
            loads[3].wait()

        def gates(j, carry):
            part = pl.ds(pl.multiple_of(j * 512, 512), 512)
            gate = dot(norm_ffn[l], wg[:, part])
            upper = dot(norm_ffn[l], wu[:, part])
            s = 0.5 * jnp.tanh(0.5 * gate) + 0.5
            swish = gate * s
            inner[l, :, part] = (swish * upper).astype(BF16)
            fact_a[l, :, part] = (upper * s * (1.0 + gate * (1.0 - s))).astype(BF16)
            fact_b[l, :, part] = swish.astype(BF16)
            return carry

        lax.fori_loop(0, ff // 512, gates, 0)

        @pl.when(l == 0)
        def _():
            loads[4].wait()

        op_start((1,), l)
        for at, size in tiles(width, 256):
            act[l + 1, :, at : at + size] = (
                middle[l, :, at : at + size] + dot_rt(inner[l], wd[at : at + size, :])
            ).astype(BF16)
        acts_out.start(act.at[l + 1], l)
        kv_sent(l)
        return carry

    lax.fori_loop(0, 2, forward, 0)

    in_remote(0, False).wait_recv()
    gain_v[...] = jnp.zeros_like(gain_v)
    br[...] = jnp.zeros_like(br)
    late = (6, 8)

    def backward(step, carry):
        l = 1 - step

        @pl.when(l == 0)
        def _():
            op_sent((2, 3, 4) + (late if complete else ()), 1)

        br[:, :width] = go[l + 1]
        op_start((4,), l)

        def gates(j, carry):
            part = pl.ds(pl.multiple_of(j * 512, 512), 512)
            grad_inner = dot(go[l + 1], wd[:, part])
            gg[:, part] = (grad_inner * fact_a[l, :, part].astype(F32)).astype(BF16)
            gu[:, part] = (grad_inner * fact_b[l, :, part].astype(F32)).astype(BF16)
            return carry

        lax.fori_loop(0, ff // 512, gates, 0)
        op_start((2, 3), l)
        for at, size in tiles(width, 256):
            sum_acc[:, at : at + size] = dot_rt(gg[...], wg[at : at + size, :]) + dot_rt(
                gu[...], wu[at : at + size, :]
            )
        grad, gain_row = norm_back(middle[l], gain_ffn, sum_acc[...])
        gain_v[1:2, :] += gain_row
        gm[...] = go[l + 1].astype(F32) + grad
        ra[1] = gm[...].astype(BF16)

        for at, size in tiles(width, 256):
            product = dot_rt(ra[1], wo[at : at + size, :])
            for inside, part in tiles(size, 128):
                block = wide(product[:, inside : inside + part])
                head = (at + inside) // HEAD_SIZE
                qd[l, head // SHARE, pl.ds((SHARE + head % SHARE) * rows, rows), :] = jnp.where(
                    low, 0.0, pltpu.roll(block, 64, 1)
                ).astype(BF16)
                head += 1
                if head < QUERY_HEADS:
                    qd[l, head // SHARE, pl.ds((SHARE + head % SHARE) * rows, rows), :] = (
                        jnp.where(low, 0.0, block).astype(BF16)
                    )

        def attention():
            back = AttentionBack(
                rank, device_of, qd.at[l], kv.at[l], o_raw.at[l], allowed_add, cos_sin, ra, pds,
                dkv, dkv_in.at[l] if complete else dkv_in, gkv,
                dk_send.at[l] if complete else dk_send, dk_recv.at[l] if complete else dk_recv,
            )
            back.heads(0, KEY_VALUE_HEADS)
            back.relay(KEY_VALUE_HEADS - 1)
            back.queries()
            op_start((6,), l)
            back.collect()
            op_start((8,), l)
            back.project(sum_acc, wq, wkv)
            grad, gain_row = norm_back(act[l].astype(F32), gain_attn, sum_acc[...])
            gain_v[0:1, :] += gain_row
            go[l] = (gm[...] + grad).astype(BF16)
            grads_out.start(go.at[l], l)

        if complete:
            attention()
        else:

            @pl.when(l == 1)
            def _():
                attention()

            @pl.when(l == 1)
            def _():
                op_sent(late, 1)

        return carry

    lax.fori_loop(0, 2, backward, 0)

    gain_copy = pltpu.make_async_copy(gain_v, gain_o, kept_sem.at[7])
    gain_copy.start()
    kept_start(5, 6)
    for into_x in (True, False):

        @pl.when(section == (0 if into_x else 1))
        def _(into_x=into_x):
            for block in range(2):

                @pl.when(jnp.logical_not(in_mine(block)))
                def _(block=block):
                    in_remote(block, into_x).wait_send()

    op_sent((2, 3, 4) + (late if complete else ()), 0)
    for l in range(2):
        op_sent((0, 1, 5, 7), l)
        for kind in range(9):
            if l == 1 or complete or kind not in late:
                op_copy(kind, l, False).wait_recv()
        acts_out.sent(act.at[l + 1], l)
        if l == 1 or complete:
            grads_out.sent(go.at[l], l)
    gain_copy.wait()
    acts_out.arrived(act.at[0])
    if complete:
        grads_out.arrived(act.at[0])
    else:

        @pl.when(section == 1)
        def _():
            grads_out.arrived(act.at[0])

        for i in range(len(kept_o)):
            kept_copy(i).wait()


def run_layers(lengths, ends, frequency, gain_attn, gain_ffn, weights, complete):
    micro_count, rows, width = ends.shape[1:]
    wq, wk, wv, wo, wg, wu, wd = weights
    ff = wg.shape[1]
    keys = RANKS * rows
    kv_width = 2 * wk.shape[0]
    vmem, hbm = pl.BlockSpec(memory_space=pltpu.VMEM), pl.BlockSpec(memory_space=pl.ANY)
    op_rows = 4 * rows
    late_rows = op_rows if complete else 2 * rows
    out = lambda *shape: jax.ShapeDtypeStruct(shape, BF16)
    out_f = lambda *shape: jax.ShapeDtypeStruct(shape, F32)
    dma = lambda *shape: pltpu.SemaphoreType.DMA(shape)
    kept = [
        out(rows, width),
        out(KEY_VALUE_HEADS, keys, 128),
        out_f(QUERY_HEADS, rows, 128),
        out_f(2, rows, 128),
        out_f(rows, keys),
        out(KEY_VALUE_HEADS, 2 * SHARE * rows, 128),
        out_f(rows, width),
    ]
    layers = (2,) if complete else ()
    return pl.pallas_call(
        lambda *refs: layers_kernel(complete, *refs),
        out_shape=[
            out(*ends.shape),
            out(*ends.shape),
            out_f(8, width),
            out(op_rows, width),
            out(op_rows, ff),
            out(op_rows, ff // 2),
            out(op_rows, ff // 2),
            out(op_rows, 512),
            out(op_rows, width),
            out(late_rows, width),
            out(op_rows, width),
            out(late_rows, 384),
        ]
        + ([] if complete else kept),
        in_specs=[pl.BlockSpec(memory_space=pltpu.SMEM), hbm] + [vmem] * 3 + [hbm] * 7,
        out_specs=[hbm] * (12 if complete else 19),
        scratch_shapes=[
            pltpu.VMEM(wq.shape, BF16),
            pltpu.VMEM((kv_width, width), BF16),
            pltpu.VMEM(wo.shape, BF16),
            pltpu.VMEM(wg.shape, BF16),
            pltpu.VMEM(wu.shape, BF16),
            pltpu.VMEM(wd.shape, BF16),
            pltpu.VMEM((3, rows, width), BF16),
            pltpu.VMEM((3, rows, width), BF16),
            pltpu.VMEM((2, rows, width), F32),
            pltpu.VMEM((2, rows, width), BF16),
            pltpu.VMEM((2, rows, ff), BF16),
            pltpu.VMEM((2, rows, ff), BF16),
            pltpu.VMEM((2, rows, ff), BF16),
            pltpu.VMEM((2, 2, rows, width), BF16),
            pltpu.VMEM((2, KEY_VALUE_HEADS, 2 * SHARE * rows, 128), BF16),
            pltpu.VMEM((2, KEY_VALUE_HEADS, keys, 128), BF16),
            pltpu.VMEM((2, QUERY_HEADS, rows, 128), F32),
            pltpu.VMEM((rows, width), F32),
            pltpu.VMEM((rows, width), F32),
            pltpu.VMEM((rows, ff), BF16),
            pltpu.VMEM((rows, ff), BF16),
            pltpu.VMEM((rows, 1024), BF16),
            pltpu.VMEM((2, rows, width), BF16),
            pltpu.VMEM((2 * SHARE * rows, keys), BF16),
            pltpu.VMEM((KEY_VALUE_HEADS, keys, 128), BF16),
            pltpu.VMEM(layers + (KEY_VALUE_HEADS, 3 * rows, 128), BF16),
            pltpu.VMEM((rows, kv_width), BF16),
            pltpu.VMEM((2, rows, 128), F32),
            pltpu.VMEM((rows, keys), F32),
            pltpu.VMEM((8, width), F32),
            dma(5),
            dma(2, KEY_VALUE_HEADS),
            dma(2),
            dma(2),
            dma(2, 3, KEY_VALUE_HEADS),
            dma(2, 3, KEY_VALUE_HEADS),
            dma(*layers, 2, KEY_VALUE_HEADS),
            dma(*layers, 3, KEY_VALUE_HEADS),
            dma(2),
            dma(2),
            dma(2),
            dma(2),
            dma(9, 2),
            dma(9, 2),
            dma(9, 2),
            dma(len(kept) + 1),
        ],
        compiler_params=pltpu.CompilerParams(
            collective_id=1, has_side_effects=True, vmem_limit_bytes=61 * 2**20
        ),
        name="layers",
    )(lengths, ends, frequency, gain_attn, gain_ffn, *weights)


MIDDLE_ORDER = (
    "near1", "near0", "head0", "head1", "head2", "far1", "head3", "head4",
    "near3", "query0", "down0", "near2", "down1", "fadd1", "far0", "aend0",
    "tready0", "tnear2", "down2", "down3", "tnear0", "down4", "far3", "down5",
    "far2", "fadd0", "tfar0", "tnear3", "dfirst0", "tnear1", "fz0", "fadd3",
    "tfar3", "tadd0", "fadd2", "fz1", "dsecond0", "fz2", "tfar1", "tfar2",
    "tadd3", "tz0", "tadd1", "ftotal0", "dgather0", "tadd2", "tz1", "tz2",
    "fmiddle0", "ttotal0", "dmiddle0",
)
END_ORDER = (
    "near1", "head0", "near0", "down0", "far1", "head1", "down1", "down2",
    "head2", "head3", "head4", "near3", "down3", "far0", "fadd1", "down4",
    "query0", "near2", "aend0", "down5", "fadd0", "far3", "fz0", "tready0",
    "tnear3", "far2", "fadd3", "tnear0", "fz2", "tnear2", "fadd2", "fz1",
    "tnear1", "tfar3", "tfar0", "dfirst0", "tfar2", "tfar1", "tadd0", "tadd3",
    "tz0", "tadd1", "dsecond0", "tz2", "ftotal0", "tadd2", "tz1", "dgather0",
    "ttotal0", "fmiddle0", "dmiddle0",
)


def sums_kernel(*refs):
    refs = list(refs)

    def take(count):
        taken = refs[:count]
        del refs[:count]
        return taken

    gain_h, gain_a, nf_h, in_h, gg_h, gu_h, br_h, la_h, ra_h, nr_h, kvg_h = take(11)
    act_h, kv_h, o_h, cs_h, allowed_h, qd_h, gm_h, wq_h, wk_h, wv_h = take(10)
    grads_o, t_o, gate_o, up_o, down_o = take(5)
    stage, in_v, br_v, gg_v, gu_v, ra_v, kvg_v, nf_t, ln_t, in_t, gain_t = take(11)
    act, kv, o_raw, cos_sin, allowed, qd, gm, wq, wkv = take(9)
    go, ra, dkv, dkv_in, gkv, sum_acc, gain_rows = take(7)
    d_out, d_in, d_keep, d1_out, d1_in, d2_out, d2_in = take(7)
    f1_out, f1_in, f2_out, f2_in, f_keep, fz_in = take(6)
    t1_out, t1_in, t2_out, t2_in, t_keep, tz_in = take(6)
    d_all, f_all, t_all = take(3)
    load, kept_sem, w_sem, dk_s, dk_r, grad_s, grad_r, op_own, op_s, op_r = take(10)
    dz_s, dz_r, d1_s, d1_r, d2_s, d2_r, f1_s, f1_r, f2_s, f2_r, fz_s, fz_r = take(12)
    t1_s, t1_r, t2_s, t2_r, tz_s, tz_r, all_s, all_r, pair_r, write = take(10)

    section = lax.axis_index("section")
    z = lax.axis_index("dp")
    ctx = lax.axis_index("ctx")
    x, y = ctx % 2, ctx // 2
    rank = 2 * section + x
    x_next = (section, z, 2 * y + 1 - x)
    y_next = (section, z, 2 * (1 - y) + x)
    partner = (1 - section, z, ctx)
    rows = act.shape[0]
    width = nf_h.shape[1]
    per = width // RANKS
    part = f_keep.shape[2]
    shift = per - part
    quarter = gg_v.shape[1] // 2
    deep = in_t.shape[0]
    fine = deep // 2
    last = RANKS - 1
    edge = ((z == 0) | (z == last)).astype(jnp.int32)

    def pick(index, values):
        if isinstance(index, int):
            return values[index]
        return sum((index == i).astype(jnp.int32) * v for i, v in enumerate(values) if not (type(v) is int and v == 0))

    def remote(src, dst, send, recv, device):
        return pltpu.make_async_remote_copy(
            src_ref=src, dst_ref=dst, send_sem=send, recv_sem=recv,
            device_id=device, device_id_type=MESH,
        )

    def some(start, size, unit=16):
        return pl.ds(pl.multiple_of(start, unit), size)

    gain_load = pltpu.make_async_copy(gain_h, gain_rows.at[pl.ds(0, gain_h.shape[0])], load.at[7])
    by_need = ((3, 2, 1, 0), (3, 0, 2, 1), (0, 3, 1, 2), (0, 1, 2, 3))
    by_turns = ((3, 2, 1, 0), (3, 0, 2, 1), (0, 3, 1, 2), (0, 2, 1, 3))

    def turn_of(k, order=by_need):
        return pick(k, [pick(z, [row[i] for row in order]) for i in range(RANKS)])

    def in_load(k):
        return pltpu.make_async_copy(
            in_h.at[:, some(turn_of(k) * deep, deep, 128)], in_v, load.at[0]
        )

    loads = [None] + [
        pltpu.make_async_copy(h, v, load.at[1 + i])
        for i, (h, v) in enumerate(
            [(br_h, br_v), (nf_h, stage), (gg_h, gg_v), (gu_h, gu_v), (la_h, stage), (nr_h, stage)]
        )
    ]
    kept = [
        pltpu.make_async_copy(h, v, kept_sem.at[i])
        for i, (h, v) in enumerate(
            [(qd_h, qd), (kv_h, kv), (o_h, o_raw), (allowed_h, allowed), (cs_h, cos_sin),
             (gm_h, gm), (act_h, act)]
        )
    ]
    late = [
        pltpu.make_async_copy(h.at[pl.ds(c * rows, rows)], v.at[pl.ds((2 * c + 1) * rows, rows)], w_sem.at[i, c])
        for i, (h, v) in enumerate([(ra_h, ra_v), (kvg_h, kvg_v)])
        for c in range(2)
    ]
    weights = [pltpu.make_async_copy(wq_h, wq, w_sem.at[2, 0])] + [
        pltpu.make_async_copy(
            h.at[pl.ds(g * HEAD_SIZE, HEAD_SIZE)],
            wkv.at[pl.ds((2 * g + i) * HEAD_SIZE, HEAD_SIZE)],
            w_sem.at[3 + i, g],
        )
        for g in range(KEY_VALUE_HEADS)
        for i, h in enumerate((wk_h, wv_h))
    ]
    loads[2].start()
    loads[3].start()
    loads[4].start()
    gain_rows[...] = jnp.zeros_like(gain_rows)

    barrier = pltpu.get_barrier_semaphore()
    greet(barrier, z)
    not_first = (z > 0).astype(jnp.int32)
    not_last = (z < last).astype(jnp.int32)

    @pl.when(z > 0)
    def _():
        pl.semaphore_signal(barrier, inc=1, device_id=(section, z - 1, ctx), device_id_type=MESH)

    @pl.when(z < last)
    def _():
        pl.semaphore_signal(barrier, inc=1, device_id=(section, z + 1, ctx), device_id_type=MESH)

    def turn(src, dst, base=0):
        for at, size in tiles(src.shape[1], 128):
            block = src[:, at : at + size]
            if size < 128:
                block = wide(block)
            dst[base + at : base + at + size, :] = block.T[:size]

    def z_way(t):
        up = (z < t).astype(jnp.int32)
        to = z + 2 * up - 1
        arrives = up * not_first + (1 - up) * not_last
        meets = (1 - up) * (t == z - 1).astype(jnp.int32)
        return (section, to, ctx), arrives, t * (1 - meets) + RANKS * meets

    def d_block(k):
        in_load(k).wait()
        for b in range(deep // 128):
            in_t[b * 128 : (b + 1) * 128, :] = in_v[:, b * 128 : (b + 1) * 128].T

        if not isinstance(k, int):

            @pl.when(k < last)
            def _():
                in_load(k + 1).start()

    def d_send(k, sub):
        device, _, slot = z_way(turn_of(k))
        span = some(sub * fine, fine)
        return remote(d_out.at[k, span], d_in.at[slot, span], dz_s.at[k, sub], dz_r.at[slot, sub], device)

    def d_step(n):
        k, sub = n // 2, n % 2

        @pl.when(n == 0)
        def _():
            loads[1].wait()

        @pl.when(sub == 0)
        def _():
            d_block(k)

        t = turn_of(k)
        _, arrives, _ = z_way(t)
        span = some(sub * fine, fine)
        mine = dot(in_t[span, :], br_v[...])

        @pl.when(arrives == 0)
        def _():
            d_out[k, span, :] = mine.astype(BF16)

        @pl.when(arrives == 1)
        def _():
            remote(d_out.at[k, span], d_in.at[t, span], dz_s.at[k, sub], dz_r.at[t, sub], partner).wait_recv()
            d_out[k, span, :] = (mine + d_in[t, span, :].astype(F32)).astype(BF16)

        d_send(k, sub).start()

    def f_links(k):
        return (x_next, y_next, x, y) if k == 0 else (y_next, x_next, y, x)

    def f_right(k, column_half):
        src = gg_v if k == 0 else gu_v
        return src[:, some(column_half * quarter, quarter, 128)]

    turns = (3, 0, 2, 1)

    def f1_copy(k, i):
        d = pick(i, turns)
        return remote(f1_out.at[k, i % 2], f1_in.at[k, d], f1_s.at[k, i % 2], f1_r.at[k, d], f_links(k)[0])

    def f2_copy(k, i):
        d = pick(i, turns)
        return remote(f2_out.at[k, i % 2], f2_in.at[k, d], f2_s.at[k, i % 2], f2_r.at[k, d], f_links(k)[1])

    def f1_step(i):
        left = nf_t[some(pick(i, turns) * per, per), :]
        for k in range(2):
            value = dot(left, f_right(k, 1 - f_links(k)[2])).astype(BF16)

            @pl.when(i >= 2)
            def _():
                f1_copy(k, i).wait_send()

            f1_out[k, i % 2] = value
            f1_copy(k, i).start()

    def f2_step(i):
        d = pick(i, turns)
        for k in range(2):
            first, second = f_links(k)[2:]
            f1_copy(k, i).wait_recv()

            def total(which):
                return (
                    dot(nf_t[some(d * per + which * shift, part), :], f_right(k, first))
                    + f1_in[k, d, some(which * shift, part), :].astype(F32)
                ).astype(BF16)

            value = total(1 - second)

            @pl.when(i >= 2)
            def _():
                f2_copy(k, i).wait_send()

            f2_out[k, i % 2] = value
            f2_copy(k, i).start()
            f_keep[k, d] = total(second)

    def t_links(d):
        x_first = (d < RANKS // 2) * 1
        choose = lambda a, b: x_first * a + (1 - x_first) * b
        ways = [tuple(choose(a, b) for a, b in zip(*pair)) for pair in ((x_next[1:], y_next[1:]), (y_next[1:], x_next[1:]))]
        return (section, *ways[0]), (section, *ways[1]), choose(x, y), choose(y, x)

    def t_product(row, count, add, dst):
        full = width // 128 * 128
        mine = dot(ln_t[some(row, count), :], ra_v[...])
        dst[:, :full] = add(mine[:, :full], 0).astype(BF16)
        tail = jnp.concatenate([mine[:, full:], gain_t[some(row, count), width - full :]], axis=1)
        dst[:, full : full + 128] = add(tail, full).astype(BF16)
        pairs = dot(ln_t[some(width + row, count), :], kvg_v[...])
        dst[:, full + 128 :] = add(pairs, full + 128).astype(BF16)

    def t1_copy(d):
        return remote(t1_out.at[d], t1_in.at[d], t1_s.at[d], t1_r.at[d], t_links(d)[0])

    def t2_copy(d):
        return remote(t2_out.at[d], t2_in.at[d], t2_s.at[d], t2_r.at[d], t_links(d)[1])

    def t1_step(d):
        first = t_links(d)[2]
        t_product(d * per + (1 - first) * shift, part, lambda v, at: v, t1_out.at[d])
        t1_copy(d).start()

    def t2_step(d):
        _, _, first, second = t_links(d)
        t1_copy(d).wait_recv()
        for which, dst in ((1 - second, t2_out), (second, t_keep)):
            row = which * (part // 2)
            add = lambda v, at: v + t1_in[d, some(row, part // 2), at : at + v.shape[1]].astype(F32)
            t_product(d * per + first * shift + row, part // 2, add, dst.at[d])
            if dst is t2_out:
                t2_copy(d).start()

    class Line:
        def __init__(self, keep, second_in, z_in, send, recv):
            self.keep, self.second_in, self.z_in, self.send, self.recv = keep, second_in, z_in, send, recv

        def add(self, copy, d):
            copy.wait_recv()
            self.keep[d] = (self.keep[d].astype(F32) + self.second_in[d].astype(F32)).astype(BF16)

        def copy(self, k):
            d = turn_of(k, by_turns)
            device, _, slot = z_way(d)
            return remote(self.keep.at[d], self.z_in.at[slot], self.send.at[k], self.recv.at[slot], device)

        def step(self, k):
            d = turn_of(k, by_turns)
            _, arrives, _ = z_way(d)

            @pl.when(arrives == 1)
            def _():
                remote(self.keep.at[d], self.z_in.at[d], self.send.at[k], self.recv.at[d], partner).wait_recv()
                self.keep[d] = (self.keep[d].astype(F32) + self.z_in[d].astype(F32)).astype(BF16)

            self.copy(k).start()

        def total(self):
            for condition, slot in ((z > 0, z), (z < last, RANKS)):

                @pl.when(condition)
                def _(slot=slot):
                    remote(self.keep.at[0], self.z_in.at[slot], self.send.at[0], self.recv.at[slot], partner).wait_recv()

            value = self.keep[z].astype(F32)
            return z_total(value, self.z_in[z], self.z_in[RANKS])

    def z_total(value, up, down):
        value = value + jnp.where(z > 0, up.astype(F32), 0.0)
        return value + jnp.where(z < last, down.astype(F32), 0.0)

    lines = [
        Line(f_keep.at[k], f2_in.at[k], fz_in.at[k], fz_s.at[k], fz_r.at[k]) for k in range(2)
    ] + [Line(t_keep, t2_in, tz_in, tz_s, tz_r)]

    def f_add(i):
        for k in range(2):
            lines[k].add(f2_copy(k, i), pick(i, turns))

    def t_add(d):
        lines[2].add(t2_copy(d), d)

    def f_line(k):
        lines[0].step(k)
        lines[1].step(k)

    def places(x_first):
        a, b = (1, 0) if x_first is True else (0, 1) if x_first is False else (x_first, 1 - x_first)
        spot = lambda i, j: a * (2 * i + j) + b * (2 * j + i)
        return spot(x, y), spot(1 - x, y), spot(x, 1 - y), spot(1 - x, 1 - y)

    class Gather:
        def __init__(self, number, buffer, x_first):
            self.n, self.buffer = number, buffer
            self.own, self.over_x, self.over_y, self.across = places(x_first)
            size = buffer.shape[2]
            cut = (size // 2 + 15) // 16 * 16
            self.halves = (pl.ds(0, cut), pl.ds(cut, size - cut))

        def whole(self, spot, slot, device):
            ref = self.buffer.at[section, spot]
            return remote(ref, ref, all_s.at[self.n, slot], all_r.at[self.n, slot], device)

        def relay(self, spot, half, device):
            ref = self.buffer.at[section, spot, self.halves[half]]
            return remote(ref, ref, all_s.at[self.n, 2 + half], all_r.at[self.n, 2 + half], device)

        def pair(self, core, spot, slot):
            ref = self.buffer.at[core, spot]
            return remote(ref, ref, all_s.at[self.n, 4 + slot], pair_r.at[self.n, spot], partner)

        def start(self, value):
            self.buffer[section, self.own] = value.astype(BF16)
            self.whole(self.own, 0, x_next).start()
            self.whole(self.own, 1, y_next).start()
            self.pair(section, self.own, 0).start()

        def middle(self):
            self.whole(self.over_x, 0, x_next).wait_recv()
            self.relay(self.over_x, 0, y_next).start()
            self.pair(section, self.over_x, 1).start()
            self.whole(self.over_y, 1, y_next).wait_recv()
            self.relay(self.over_y, 1, x_next).start()
            self.pair(section, self.over_y, 2).start()

        def finish(self):
            self.relay(self.across, 0, y_next).wait_recv()
            self.relay(self.across, 1, x_next).wait_recv()
            self.pair(section, self.across, 3).start()
            for spot in (self.own, self.over_x, self.over_y, self.across):
                self.pair(1 - section, spot, 0).wait_recv()

        def sent(self):
            self.whole(self.own, 0, x_next).wait_send()
            self.whole(self.own, 1, y_next).wait_send()
            self.relay(self.over_x, 0, y_next).wait_send()
            self.relay(self.over_y, 1, x_next).wait_send()
            for slot, spot in enumerate((self.own, self.over_x, self.over_y, self.across)):
                self.pair(section, spot, slot).wait_send()

    below = (z < RANKS // 2).astype(jnp.int32)
    gathers = [
        Gather(0, d_all.at[0], True),
        Gather(1, d_all.at[1], False),
        Gather(2, f_all.at[0], True),
        Gather(3, f_all.at[1], False),
        Gather(4, t_all, below),
    ]

    def d1_copy(h):
        return remote(d1_out.at[h], d1_in.at[h], d1_s.at[h], d1_r.at[h], f_links(h)[0])

    def d2_copy(h):
        return remote(d2_out.at[h], d2_in.at[h], d2_s.at[h], d2_r.at[h], f_links(h)[1])

    def d_first(h):
        span = pl.ds(h * fine, fine)
        for condition, slot in ((z > 0, z), (z < last, RANKS)):

            @pl.when(condition)
            def _(slot=slot):
                remote(d_out.at[0, span], d_in.at[slot, span], dz_s.at[0, h], dz_r.at[slot, h], partner).wait_recv()

        first = f_links(h)[2]
        for mine in (False, True):
            at = h * fine + (first if mine else 1 - first) * (fine // 2)
            piece = some(at, fine // 2)
            total = z_total(dot(in_t[piece, :], br_v[...]), d_in[z, piece, :], d_in[RANKS, piece, :])
            if mine:
                d_keep[h] = total
            else:
                d1_out[h] = total.astype(BF16)
                d1_copy(h).start()

    def d_second(h):
        second = f_links(h)[3]
        d1_copy(h).wait_recv()
        for mine in (False, True):
            piece = some((second if mine else 1 - second) * (fine // 4), fine // 4)
            total = d_keep[h, piece, :] + d1_in[h, piece, :].astype(F32)
            if mine:
                d_keep[h, : fine // 4, :] = total
            else:
                d2_out[h] = total.astype(BF16)
                d2_copy(h).start()

    def d_gather(h):
        d2_copy(h).wait_recv()
        gathers[h].start(d_keep[h, : fine // 4, :] + d2_in[h].astype(F32))

    back = AttentionBack(
        rank, lambda r: (r // 2, z, 2 * y + r % 2), qd, kv, o_raw, allowed, cos_sin, ra,
        ln_t.at[pl.ds(0, 2 * SHARE * rows)], dkv, dkv_in, gkv, dk_s, dk_r,
    )
    grads_out = OutCopy(grads_o, grad_s, grad_r)

    def op_copy(kind, own):
        role = section if own else 1 - section
        src = ra.at[role] if kind == 0 else gkv.at[:, some(role * 256, 384, 128)]
        dst = (ra_v, kvg_v)[kind].at[some(2 * section * rows, rows)]
        if own:
            return pltpu.make_async_copy(src, dst, op_own.at[kind])
        return remote(src, dst, op_s.at[kind], op_r.at[kind], partner)

    def op_start(kind):
        op_copy(kind, True).start()
        op_copy(kind, False).start()

    def attention_end():
        back.collect()
        op_start(1)
        for copy in weights:
            copy.wait()
        kept[6].wait()
        back.project(sum_acc, wq, wkv)
        grad, gain_row = norm_back(act[...].astype(F32), gain_a[...].astype(F32).reshape(1, width), sum_acc[...])
        gain_load.wait()
        gain_rows[0:1, :] += gain_row
        go[...] = (gm[...] + grad).astype(BF16)
        grads_out.start(go, 0)

    def t_ready():
        loads[5].wait()
        turn(stage, ln_t)
        loads[6].start()
        block_of = lambda at, size: wide(gain_rows[:, at : at + size]).T
        for at, size in tiles(width, 128):
            gain_t[at : at + size, :] = pltpu.roll(block_of(at, size), 64, 1)[:size]
        loads[6].wait()
        turn(stage, ln_t, width)
        for copy in late:
            copy.wait()
        for kind in range(2):
            op_copy(kind, True).wait()
            op_copy(kind, False).wait_recv()

    def both(step):
        step(0)
        step(1)

    def head_step(g):
        @pl.when(g == 0)
        def _():
            for copy in kept[:6]:
                copy.wait()
            ra[1] = gm[...].astype(BF16)

        back.head(g)

        @pl.when(g > 0)
        def _():
            back.relay(g - 1)

    def queries_step():
        back.relay(KEY_VALUE_HEADS - 1)
        back.queries()
        op_start(0)

    def d_first_step():
        d_block(last)
        both(d_first)

    def f_total():
        both(lambda k: gathers[2 + k].start(lines[k].total()))

    actions = {
        "near": f1_step,
        "far": f2_step,
        "tnear": t1_step,
        "tfar": t2_step,
        "down": d_step,
        "head": head_step,
        "fadd": f_add,
        "fz": f_line,
        "tadd": t_add,
        "tz": lines[2].step,
        "query": lambda p: queries_step(),
        "aend": lambda p: attention_end(),
        "tready": lambda p: t_ready(),
        "dfirst": lambda p: d_first_step(),
        "dsecond": lambda p: both(d_second),
        "dgather": lambda p: both(d_gather),
        "ftotal": lambda p: f_total(),
        "ttotal": lambda p: gathers[4].start(lines[2].total()),
        "fmiddle": lambda p: both(lambda k: gathers[2 + k].middle()),
        "dmiddle": lambda p: both(lambda h: gathers[h].middle()),
    }
    names = list(actions)

    def codes(table):
        return [8 * names.index(step.rstrip("0123456789")) + int(step[-1]) for step in table]

    tables = [codes(MIDDLE_ORDER), codes(END_ORDER)]
    steps = max(len(t) for t in tables)

    loads[2].wait()
    turn(stage, nf_t)
    loads[3].wait()
    loads[4].wait()
    in_load(0).start()
    loads[1].start()
    for copy in kept + weights + late + [gain_load]:
        copy.start()
    pl.semaphore_wait(barrier, 7 + not_first + not_last)
    loads[5].start()

    def one(n, carry):
        code = (1 - edge) * pick(n, tables[0]) + edge * pick(n, tables[1])
        lax.switch(code // 8, list(actions.values()), code % 8)
        return carry

    lax.fori_loop(0, steps, one, 0)

    writes = []

    def leave(src, dst):
        writes.append(pltpu.make_async_copy(src, dst, write.at[len(writes)]))
        writes[-1].start()

    for k in range(2):
        gathers[2 + k].finish()
        for core in range(2):
            for f in range(2):
                columns = pl.ds((2 * core + f) * quarter, quarter)
                out = (gate_o, up_o)[k]
                leave(f_all.at[k, core, 2 * f], out.at[pl.ds(0, part), columns])
                rest = pl.ds(part - shift, per - part)
                leave(f_all.at[k, core, 2 * f + 1, rest], out.at[pl.ds(part, per - part), columns])
    gathers[4].middle()
    for h in range(2):
        gathers[h].finish()
        for core in range(2):
            for spot in range(4):
                span = pl.ds(h * fine + spot * (fine // 4), fine // 4)
                leave(d_all.at[h, core, spot], down_o.at[span, pl.ds(core * br_v.shape[1], br_v.shape[1])])
    gathers[4].finish()
    t_rows = part // 2
    for core in range(2):
        for spot in range(4):
            row = spot % 2 * t_rows + spot // 2 * shift
            skip = part - shift if spot == 2 else 0
            rest = pl.ds(skip, t_rows - skip)
            leave(t_all.at[core, spot, rest], t_o.at[core, pl.ds(row + skip, t_rows - skip)])

    for k in range(last):
        for sub in range(2):
            d_send(k, sub).wait_send()
        for line in lines:
            line.copy(k).wait_send()
    for h in range(2):
        d1_copy(h).wait_send()
        d2_copy(h).wait_send()
    for k in range(2):
        for i in (2, 3):
            f1_copy(k, i).wait_send()
            f2_copy(k, i).wait_send()
    for d in range(RANKS):
        t1_copy(d).wait_send()
        t2_copy(d).wait_send()
    for kind in range(2):
        op_copy(kind, False).wait_send()
    grads_out.sent(go, 0)

    @pl.when(section == 0)
    def _():
        grads_out.arrived(go)

    for gather in gathers:
        gather.sent()
    for copy in writes:
        copy.wait()


def run_sums(gain_sums, gain_attn, operands, kept, weights, ends_shape):
    nf, inner, gg, gu, br, la, ra, nr, kvg = operands
    act, kv, o_raw, cos_sin, allowed, qd, gm = kept
    depth, width = nf.shape
    rows = act.shape[0]
    ff, half = inner.shape[1], gg.shape[1]
    per, deep = width // RANKS, ff // RANKS
    part = (per // 2 + 15) // 16 * 16
    quarter, fine = half // 2, deep // 2
    columns = br.shape[1]
    wide_t = width // 128 * 128 + 128 + kvg.shape[1]
    vmem, hbm = pl.BlockSpec(memory_space=pltpu.VMEM), pl.BlockSpec(memory_space=pl.ANY)
    out = lambda *shape: jax.ShapeDtypeStruct(shape, BF16)
    b = lambda *shape: pltpu.VMEM(shape, BF16)
    f = lambda *shape: pltpu.VMEM(shape, F32)
    like = lambda a: pltpu.VMEM(a.shape, a.dtype)
    sem = lambda *shape: pltpu.SemaphoreType.DMA(shape)
    return pl.pallas_call(
        sums_kernel,
        out_shape=[
            out(*ends_shape), out(2, per, wide_t), out(per, ff), out(per, ff), out(deep, 2 * columns),
        ],
        in_specs=[hbm, vmem] + [hbm] * 19,
        out_specs=[hbm] * 5,
        scratch_shapes=[
            b(depth, width), b(depth, deep), b(depth, columns), b(depth, half), b(depth, half),
            b(depth, width), b(depth, kvg.shape[1]),
            b(width, depth), b(2 * width, depth), b(deep, depth), f(width, 128),
            like(act), like(kv), like(o_raw), like(cos_sin), like(allowed), like(qd), like(gm),
            like(weights[0]), b(2 * weights[1].shape[0], width),
            b(rows, width), b(2, rows, width), like(kv), b(KEY_VALUE_HEADS, 3 * rows, 128), b(rows, KEY_VALUE_HEADS * 128),
            f(rows, width), f(128, width),
            b(RANKS - 1, deep, columns), b(5, deep, columns), f(2, fine // 2, columns),
            b(2, fine // 2, columns), b(2, fine // 2, columns), b(2, fine // 4, columns), b(2, fine // 4, columns),
            b(2, 2, per, quarter), b(2, RANKS, per, quarter),
            b(2, 2, part, quarter), b(2, RANKS, part, quarter), b(2, RANKS, part, quarter), b(2, 5, part, quarter),
            b(RANKS, part, wide_t), b(RANKS, part, wide_t),
            b(RANKS, part // 2, wide_t), b(RANKS, part // 2, wide_t), b(RANKS, part // 2, wide_t), b(5, part // 2, wide_t),
            b(2, 2, 4, fine // 4, columns), b(2, 2, 4, part, quarter), b(2, 4, part // 2, wide_t),
            sem(8), sem(7), sem(5, KEY_VALUE_HEADS), sem(2, KEY_VALUE_HEADS), sem(3, KEY_VALUE_HEADS), sem(2), sem(2), sem(2), sem(2), sem(2),
            sem(3, 2), sem(5, 2), sem(2), sem(2), sem(2), sem(2),
            sem(2, 2), sem(2, 4), sem(2, 2), sem(2, 4), sem(2, 3), sem(2, 5),
            sem(4), sem(4), sem(4), sem(4), sem(3), sem(5),
            sem(5, 8), sem(5, 4), sem(5, 4), sem(40),
        ],
        compiler_params=pltpu.CompilerParams(
            collective_id=2, has_side_effects=True, vmem_limit_bytes=61 * 2**20
        ),
        name="sums",
    )(gain_sums, gain_attn, *operands, *kept, *weights)


def finish_kernel(
    acts_h, first_h, second_h, t_h, gate_h, up_h, down_h,
    acts_o, grads_o, q_o, out_o, key_o, value_o, gain_a, gain_f, gate_o, up_o, down_o,
    row_v, t_v, gate_v, down_v, q_f, kv_f, gate_f, down_f, load, store,
):
    width = q_f.shape[2]
    loads = [
        pltpu.make_async_copy(h, v, load.at[i])
        for i, (h, v) in enumerate(
            [(gate_h, gate_v.at[0]), (up_h, gate_v.at[1]), (down_h, down_v), (t_h, t_v), (acts_h, row_v.at[0])]
        )
    ]
    stores = [
        pltpu.make_async_copy(v, h, store.at[i])
        for i, (v, h) in enumerate(
            [(row_v.at[0], acts_o), (row_v.at[1], grads_o), (gate_f.at[0], gate_o), (gate_f.at[1], up_o),
             (down_f, down_o), (q_f.at[0], q_o), (q_f.at[1], out_o), (kv_f.at[0], key_o), (kv_f.at[1], value_o)]
        )
    ]
    section = lax.axis_index("section")
    for copy in loads:
        copy.start()
    start_if(
        section == 0,
        lambda: pltpu.make_async_copy(first_h, row_v.at[1], load.at[5]),
        lambda: pltpu.make_async_copy(second_h, row_v.at[1], load.at[5]),
    )
    for k in range(2):
        loads[k].wait()
        gate_f[k] = gate_v[k].astype(F32)
        stores[2 + k].start()
    loads[4].wait()
    stores[0].start()
    pltpu.make_async_copy(first_h, row_v.at[1], load.at[5]).wait()
    stores[1].start()
    loads[2].wait()
    for at, size in tiles(width, 128):
        down_f[at : at + size, :] = down_v[:, at : at + 128].astype(F32).T[:size]
    stores[4].start()
    loads[3].wait()
    for core in range(2):
        q_f[core] = t_v[core, :, :width].astype(F32)
        stores[5 + core].start()
    pairs_at = width // 128 * 128 + 128
    half = KEY_VALUE_HEADS // 2 + 1
    for g in range(KEY_VALUE_HEADS):
        core = 0 if g < half else 1
        at = pairs_at + (g - core * (KEY_VALUE_HEADS - half)) * 128
        block = t_v[core, :, at : at + 128].astype(F32).T
        kv_f[0, g * HEAD_SIZE : (g + 1) * HEAD_SIZE, :] = block[:HEAD_SIZE]
        kv_f[1, g * HEAD_SIZE : (g + 1) * HEAD_SIZE, :] = block[HEAD_SIZE:]
    for copy in stores[7:]:
        copy.start()
    tail = slice(pairs_at - 128, pairs_at)
    both = t_v[0, :, tail].astype(F32) + t_v[1, :, tail].astype(F32)
    row = width % 128
    gain_rows = both.T
    gain_a[...] = gain_rows[row]
    gain_f[...] = gain_rows[row + 1]
    for copy in stores:
        copy.wait()


def run_finish(acts, grads_first, grads_second, t_sum, gate, up, down, width):
    per, ff = gate.shape
    vmem, hbm = pl.BlockSpec(memory_space=pltpu.VMEM), pl.BlockSpec(memory_space=pl.ANY)
    out = lambda *shape: jax.ShapeDtypeStruct(shape, F32)
    kv_rows = KEY_VALUE_HEADS * HEAD_SIZE
    return pl.pallas_call(
        finish_kernel,
        out_shape=[
            jax.ShapeDtypeStruct(acts.shape, BF16), jax.ShapeDtypeStruct(acts.shape, BF16),
            out(per, width), out(per, width), out(kv_rows, per), out(kv_rows, per), out(per), out(per),
            out(per, ff), out(per, ff), out(width, down.shape[0]),
        ],
        in_specs=[hbm] * 7,
        out_specs=[hbm] * 6 + [vmem] * 2 + [hbm] * 3,
        scratch_shapes=[
            pltpu.VMEM((2, *acts.shape), BF16), pltpu.VMEM(t_sum.shape, BF16), pltpu.VMEM((2, per, ff), BF16), pltpu.VMEM(down.shape, BF16),
            pltpu.VMEM((2, per, width), F32), pltpu.VMEM((2, kv_rows, per), F32),
            pltpu.VMEM((2, per, ff), F32), pltpu.VMEM((width, down.shape[0]), F32),
            pltpu.SemaphoreType.DMA((6,)), pltpu.SemaphoreType.DMA((9,)),
        ],
        compiler_params=pltpu.CompilerParams(vmem_limit_bytes=61 * 2**20),
        name="finish",
    )(acts, grads_first, grads_second, t_sum, gate, up, down)


def sums_by_xla(gain_sums, operands):
    nf, inner, gg, gu, br, la, ra, nr, kvg = operands
    width = nf.shape[1]

    def reduced(left, right):
        total = dot_lt(left, right).astype(BF16)
        piece = lax.psum_scatter(total, "dp", scatter_dimension=0, tiled=True)
        return lax.psum(piece, "ctx")

    def both(piece, axis):
        return lax.all_gather(piece, "section", axis=axis, tiled=axis > 0).astype(F32)

    attn = both(reduced(la, ra), 0)
    gain_sum = lax.psum(gain_sums[:2], ("section", "ctx"))
    return (
        attn[0],
        attn[1],
        both(reduced(nr, kvg), 0),
        lax.psum_scatter(gain_sum, "dp", scatter_dimension=1, tiled=True),
        both(reduced(nf, gg), 1),
        both(reduced(nf, gu), 1),
        both(reduced(inner, br), 1)[:, :width],
    )


def shards(
    ends,
    doc_lengths,
    w_query,
    key_projection_weight,
    value_projection_weight,
    w_out,
    w_gate,
    w_up,
    w_down,
    gain_attn,
    gain_ffn,
):
    width = ends.shape[3]
    half = HEAD_SIZE // 2
    turns = np.float32(10000.0) ** (
        np.float32(-2.0) * (np.arange(128) % half).astype(np.float32) / np.float32(HEAD_SIZE)
    )
    weights = (
        w_query,
        key_projection_weight.T,
        value_projection_weight.T,
        w_out,
        w_gate,
        w_up,
        w_down.T,
    )
    ff = w_gate.shape[1]
    fits = lax.axis_size("dp") == RANKS and width % 64 == 0 and ff % 1280 == 0
    acts, grads_in, gain_sums, *kept = run_layers(
        doc_lengths,
        ends,
        jnp.asarray(turns.reshape(1, 128), F32),
        gain_attn,
        gain_ffn,
        weights,
        not fits,
    )
    operands = kept[:9]
    if fits:
        grads_first, *sums = run_sums(
            gain_sums, gain_attn, operands, kept[9:], weights[:3], ends.shape
        )
        acts, grads_in, grad_query, grad_out, grad_key, grad_value, *gain_piece, grad_gate, grad_up, grad_down = (
            run_finish(acts, grads_first, grads_in, *sums, width)
        )
        grad_key, grad_value, grad_down = grad_key.T, grad_value.T, grad_down.T
    else:
        grad_query, grad_out, kv_parts, gain_piece, grad_gate, grad_up, grad_down = sums_by_xla(
            gain_sums, operands
        )
        kv_grad = jnp.concatenate([kv_parts[0], kv_parts[1][:, 128:]], axis=1).reshape(
            -1, KEY_VALUE_HEADS, 2, HEAD_SIZE
        )
        grad_key = kv_grad[:, :, 0].reshape(kv_grad.shape[0], -1)
        grad_value = kv_grad[:, :, 1].reshape(kv_grad.shape[0], -1)
    return (
        acts,
        grads_in,
        grad_query,
        grad_key,
        grad_value,
        grad_out,
        grad_gate,
        grad_up,
        grad_down,
        gain_piece[0],
        gain_piece[1],
    )


def solution(mesh):
    return jax.shard_map(
        shards,
        mesh=mesh,
        in_specs=(P("section", None, ("dp", "ctx"), None), P(None, "dp", None)) + (P(),) * 9,
        out_specs=(P("section", None, ("dp", "ctx"), None),) * 2
        + (P("dp", None),) * 7
        + (P("dp"),) * 2,
        check_vma=False,
    )
```

profile of v0, /device:TPU:0, one launch (start us, length us, event | category | flops | bytes accessed | tf_op | source)
XLA Modules:
  0.0 201.8 jit_solution(9899867143389740737)
XLA Ops:
  0.6 75.8 %layers.1 = (bf16[1,2,224,960]{3,2,1,0:T(8,128)(2,1)}, bf16[1,2,224,960]{3,2,1,0:T(8,128)(2,1)}, f32[8,960]{1,0:T(8,128)}, bf16[896,960]{1,0:T(8,128)(2,1)}, bf1...) custom-call(s32[2,1,2]{2,1,0:T(1,128)} %refs_0_.1, ...), custom_call_target="tpu_custom_call" | custom-call | tf_op jit(solution)/shard_map/layers/pallas_call | solution.py:712
  76.5 117.3 %sums.1 = (bf16[1,2,224,960]{3,2,1,0:T(8,128)(2,1)}, bf16[2,240,1408]{2,1,0:T(8,128)(2,1)}, bf16[240,2560]{1,0:T(8,128)(2,1)}, bf16[240,2560]{1,0:T(8,128)(2,1)}, bf16[640,1024]{1,0:T(8,128)(2,1)}) custom-call(f32[8,960]{1,0:T(8,128)} %get-tuple-element.47.refs_0_, bf16[960]{0:T(1024)(128)(2,1)} %refs_1_.3, bf16[896,960]{1,0:T(8,128)(2,1)} %get-tuple-element.48.refs_2_, ...), custom_call_target="tpu_custom_call" | custom-call | tf_op jit(solution)/shard_map/sums/pallas_call | solution.py:1419
  193.8 7.8 %finish.1 = (bf16[1,2,224,960]{3,2,1,0:T(8,128)(2,1)}, bf16[1,2,224,960]{3,2,1,0:T(8,128)(2,1)}, f32[240,960]{1,0:T(8,128)}, f32[240,960]{1,0:T(8,128)}, f32[320...) custom-call(bf16[1,2,224,960]{3,2,1,0:T(8,128)(2,1)} %get-tuple-elem, ...), custom_call_target="tpu_custom_call" | custom-call | tf_op jit(solution)/shard_map/finish/pallas_call | solution.py:1522
where the time goes:
time: 202 us
  Pallas kernels  201 us (100%)
    pallas_call x1, Pallas kernels, run_sums(): pl.pallas_call(sums_kernel, out_shape=[out(*ends_shape), out(2, per, wide...  117 us
    pallas_call x1, Pallas kernels, run_layers(): pl.pallas_call(lambda *refs: layers_kernel(complete, *refs), out_shape=[o...  75.8 us
    pallas_call x1, Pallas kernels, run_finish(): pl.pallas_call(finish_kernel, out_shape=[jax.ShapeDtypeStruct(acts.shape,...  7.76 us

commit v1 on v0

--- a/solution.py
+++ b/solution.py
@@ -89,18 +89,18 @@
     def head(self, g):
         rows = self.rows
         kv_g = self.kv[g]
-        for i in range(SHARE):
-            mine = slice(i * rows, (i + 1) * rows)
-            other = slice((SHARE + i) * rows, (SHARE + i + 1) * rows)
+        mine = [slice(i * rows, (i + 1) * rows) for i in range(SHARE)]
+        other = [slice((SHARE + i) * rows, (SHARE + i + 1) * rows) for i in range(SHARE)]
+        all_scores = [dot_rt(self.qd[g, span, :], kv_g) + self.allowed[...] for span in mine]
+        for i, scores in enumerate(all_scores):
             kept = self.o_raw[g * SHARE + i]
-            scores = dot_rt(self.qd[g, mine, :], kv_g) + self.allowed[...]
             probs = jnp.exp(scores - kept[:, 0:1])
-            grad_out = self.qd[g, other, :]
+            grad_out = self.qd[g, other[i], :]
             grad_probs = dot_rt(grad_out, kv_g)
             weight = jnp.sum(grad_out.astype(F32) * kept, axis=-1, keepdims=True)
             grad_scores = (probs * (grad_probs - weight)).astype(BF16)
-            self.pds[mine, :] = grad_scores
-            self.pds[other, :] = probs.astype(BF16)
+            self.pds[mine[i], :] = grad_scores
+            self.pds[other[i], :] = probs.astype(BF16)
             self.o_raw[g * SHARE + i] = dot(grad_scores, kv_g)
         grad_kv = dot_lt(self.qd[g], self.pds[...])
         self.dkv[g] = grad_kv.T.astype(BF16)
@@ -361,7 +361,7 @@
     )
 
     def kv_rows(l, r, g):
-        return kv.at[l, g, pl.ds(r * rows, rows)]
+        return kv.at[l, g, pl.ds(pl.multiple_of(r * rows, 16), rows)]
 
     def kv_copy(l, quarter, dst, slot, g):
         return pltpu.make_async_remote_copy(
@@ -373,15 +373,14 @@
             device_id_type=MESH,
         )
 
-    kv_plan = [(0, 0, 1, 0), (0, 0, 2, 1), (1, 1, 2, 0), (1, 1, 3, 1), (2, 2, 3, 0)]
-    kv_relay = (1, 0, 3, 2)
-
     def kv_start(l, g):
-        for sender, quarter, dst, slot in kv_plan:
-
-            @pl.when(rank == sender)
-            def _(quarter=quarter, dst=dst, slot=slot):
-                kv_copy(l, quarter, dst, slot, g).start()
+        @pl.when(rank < 3)
+        def _():
+            kv_copy(l, rank, rank + 1, 0, g).start()
+
+        @pl.when(rank < 2)
+        def _():
+            kv_copy(l, rank, rank + 2, 1, g).start()
 
     def kv_relayed(l, g):
         @pl.when(rank == 1)
@@ -390,21 +389,27 @@
             kv_copy(l, 0, 3, 2, g).start()
 
     def kv_finish(l, g):
-
-        for quarter, receivers in ((0, (2, 3)), (1, (2, 3)), (2, (3,))):
-            for receiver in receivers:
-
-                @pl.when(rank == receiver)
-                def _(quarter=quarter):
-                    kv_copy(l, quarter, 0, 0, g).wait_recv()
+        @pl.when(rank >= 2)
+        def _():
+            kv_copy(l, 0, 0, 0, g).wait_recv()
+            kv_copy(l, 1, 0, 0, g).wait_recv()
+
+        @pl.when(rank == 3)
+        def _():
+            kv_copy(l, 2, 0, 0, g).wait_recv()
 
     def kv_sent(l):
-        for sender, quarter, dst, slot in kv_plan + [kv_relay]:
-
-            @pl.when(rank == sender)
-            def _(quarter=quarter, dst=dst, slot=slot):
+        for senders, slot in ((3, 0), (2, 1)):
+
+            @pl.when(rank < senders)
+            def _(slot=slot):
                 for g in range(KEY_VALUE_HEADS):
-                    kv_copy(l, quarter, dst, slot, g).wait_send()
+                    kv_copy(l, rank, rank + 1 + slot, slot, g).wait_send()
+
+        @pl.when(rank == 1)
+        def _():
+            for g in range(KEY_VALUE_HEADS):
+                kv_copy(l, 0, 3, 2, g).wait_send()
 
     acts_out = OutCopy(acts_o, act_send, act_recv)
     grads_out = OutCopy(grads_o, grad_send, grad_recv)
@@ -472,6 +477,7 @@
             block = dot_rt(lm[l, 0], wkv[128 * g : 128 * g + 128, :])
             turned = half_turned(block, cos_kv, sin_kv, 1.0)
             kv[l, g, mine, :] = turned.astype(BF16)
+        for g in range(KEY_VALUE_HEADS):
             kv_start(l, g)
 
         @pl.when(l == 0)
@@ -507,8 +513,11 @@
                 kv_finish(l, g)
 
             kv_g = kv[l, g]
-            for i in range(SHARE):
-                scores = dot_rt(qd[l, g, i * rows : (i + 1) * rows, :], kv_g) + allowed_add[...]
+            all_scores = [
+                dot_rt(qd[l, g, i * rows : (i + 1) * rows, :], kv_g) + allowed_add[...]
+                for i in range(SHARE)
+            ]
+            for i, scores in enumerate(all_scores):
                 peak = jnp.max(scores, axis=-1, keepdims=True)
                 exponent = jnp.exp(scores - peak)
                 total = jnp.sum(exponent, axis=-1, keepdims=True)

time: 202 us -> 197 us (0.975)
  Pallas kernels: 201 us -> 196 us
    pallas_call x1, Pallas kernels: 75.8 us -> 71.9 us  [run_layers(): pl.pallas_call(lambda *refs: layers_kernel(complete, *refs), out_shape=[o...]
where the time goes in v1:
time: 197 us
  Pallas kernels  196 us (99%)
    pallas_call x1, Pallas kernels, run_sums(): pl.pallas_call(sums_kernel, out_shape=[out(*ends_shape), out(2, per, wide...  116 us
    pallas_call x1, Pallas kernels, run_layers(): pl.pallas_call(lambda *refs: layers_kernel(complete, *refs), out_shape=[o...  71.9 us
    pallas_call x1, Pallas kernels, run_finish(): pl.pallas_call(finish_kernel, out_shape=[jax.ShapeDtypeStruct(acts.shape,...  7.76 us

profile of v1, /device:TPU:0, one launch (start us, length us, event | category | flops | bytes accessed | tf_op | source)
XLA Modules:
  0.0 196.9 jit_solution(14892669724942817227)
XLA Ops:
  0.6 71.9 %layers.1 = (bf16[1,2,224,960]{3,2,1,0:T(8,128)(2,1)}, bf16[1,2,224,960]{3,2,1,0:T(8,128)(2,1)}, f32[8,960]{1,0:T(8,128)}, bf16[896,960]{1,0:T(8,128)(2,1)}, bf1...) custom-call(s32[2,1,2]{2,1,0:T(1,128)} %refs_0_.1, ...), custom_call_target="tpu_custom_call" | custom-call | tf_op jit(solution)/shard_map/layers/pallas_call | solution.py:721
  72.5 116.5 %sums.1 = (bf16[1,2,224,960]{3,2,1,0:T(8,128)(2,1)}, bf16[2,240,1408]{2,1,0:T(8,128)(2,1)}, bf16[240,2560]{1,0:T(8,128)(2,1)}, bf16[240,2560]{1,0:T(8,128)(2,1)}, bf16[640,1024]{1,0:T(8,128)(2,1)}) custom-call(f32[8,960]{1,0:T(8,128)} %get-tuple-element.47.refs_0_, bf16[960]{0:T(1024)(128)(2,1)} %refs_1_.3, bf16[896,960]{1,0:T(8,128)(2,1)} %get-tuple-element.48.refs_2_, ...), custom_call_target="tpu_custom_call" | custom-call | tf_op jit(solution)/shard_map/sums/pallas_call | solution.py:1428
  189.0 7.8 %finish.1 = (bf16[1,2,224,960]{3,2,1,0:T(8,128)(2,1)}, bf16[1,2,224,960]{3,2,1,0:T(8,128)(2,1)}, f32[240,960]{1,0:T(8,128)}, f32[240,960]{1,0:T(8,128)}, f32[320...) custom-call(bf16[1,2,224,960]{3,2,1,0:T(8,128)(2,1)} %get-tuple-elem, ...), custom_call_target="tpu_custom_call" | custom-call | tf_op jit(solution)/shard_map/finish/pallas_call | solution.py:1531

commit v2 on v1

--- a/solution.py
+++ b/solution.py
@@ -454,7 +454,13 @@
             op_copy(kind, l, False).wait_send()
 
     def kept_copy(i):
-        src = [act.at[0], kv.at[0], o_raw.at[0], cos_sin, allowed_add, qd.at[0], gm][i]
+        if i == 7:
+            part = pl.ds(0, SHARE * rows)
+            return pltpu.make_async_copy(qd.at[0, :, part], kept_o[5].at[:, part], kept_sem.at[8])
+        if i == 5:
+            part = pl.ds(SHARE * rows, SHARE * rows)
+            return pltpu.make_async_copy(qd.at[0, :, part], kept_o[5].at[:, part], kept_sem.at[5])
+        src = [act.at[0], kv.at[0], o_raw.at[0], cos_sin, allowed_add, None, gm][i]
         return pltpu.make_async_copy(src, kept_o[i], kept_sem.at[i])
 
     def kept_start(*which):
@@ -529,7 +535,7 @@
 
         @pl.when(l == 0)
         def _():
-            kept_start(1, 2)
+            kept_start(1, 2, 7)
             loads[1].wait()
 
         for at, size in tiles(width, 128):
@@ -552,7 +558,7 @@
             loads[3].wait()
 
         def gates(j, carry):
-            part = pl.ds(pl.multiple_of(j * 512, 512), 512)
+            part = pl.ds(pl.multiple_of(j * 1280, 128), 1280)
             gate = dot(norm_ffn[l], wg[:, part])
             upper = dot(norm_ffn[l], wu[:, part])
             s = 0.5 * jnp.tanh(0.5 * gate) + 0.5
@@ -562,7 +568,7 @@
             fact_b[l, :, part] = swish.astype(BF16)
             return carry
 
-        lax.fori_loop(0, ff // 512, gates, 0)
+        lax.fori_loop(0, ff // 1280, gates, 0)
 
         @pl.when(l == 0)
         def _():
@@ -595,13 +601,13 @@
         op_start((4,), l)
 
         def gates(j, carry):
-            part = pl.ds(pl.multiple_of(j * 512, 512), 512)
+            part = pl.ds(pl.multiple_of(j * 1280, 128), 1280)
             grad_inner = dot(go[l + 1], wd[:, part])
             gg[:, part] = (grad_inner * fact_a[l, :, part].astype(F32)).astype(BF16)
             gu[:, part] = (grad_inner * fact_b[l, :, part].astype(F32)).astype(BF16)
             return carry
 
-        lax.fori_loop(0, ff // 512, gates, 0)
+        lax.fori_loop(0, ff // 1280, gates, 0)
         op_start((2, 3), l)
         for at, size in tiles(width, 256):
             sum_acc[:, at : at + size] = dot_rt(gg[...], wg[at : at + size, :]) + dot_rt(
@@ -611,6 +617,10 @@
         gain_v[1:2, :] += gain_row
         gm[...] = go[l + 1].astype(F32) + grad
         ra[1] = gm[...].astype(BF16)
+
+        @pl.when(l == 0)
+        def _():
+            kept_start(6)
 
         for at, size in tiles(width, 256):
             product = dot_rt(ra[1], wo[at : at + size, :])
@@ -662,7 +672,7 @@
 
     gain_copy = pltpu.make_async_copy(gain_v, gain_o, kept_sem.at[7])
     gain_copy.start()
-    kept_start(5, 6)
+    kept_start(5)
     for into_x in (True, False):
 
         @pl.when(section == (0 if into_x else 1))
@@ -692,7 +702,7 @@
         def _():
             grads_out.arrived(act.at[0])
 
-        for i in range(len(kept_o)):
+        for i in range(len(kept_o) + 1):
             kept_copy(i).wait()
 
 
@@ -783,7 +793,7 @@
             dma(9, 2),
             dma(9, 2),
             dma(9, 2),
-            dma(len(kept) + 1),
+            dma(len(kept) + 2),
         ],
         compiler_params=pltpu.CompilerParams(
             collective_id=1, has_side_effects=True, vmem_limit_bytes=61 * 2**20
@@ -793,22 +803,22 @@
 
 
 MIDDLE_ORDER = (
-    "near1", "near0", "head0", "head1", "head2", "far1", "head3", "head4",
-    "near3", "query0", "down0", "near2", "down1", "fadd1", "far0", "aend0",
-    "tready0", "tnear2", "down2", "down3", "tnear0", "down4", "far3", "down5",
-    "far2", "fadd0", "tfar0", "tnear3", "dfirst0", "tnear1", "fz0", "fadd3",
-    "tfar3", "tadd0", "fadd2", "fz1", "dsecond0", "fz2", "tfar1", "tfar2",
-    "tadd3", "tz0", "tadd1", "ftotal0", "dgather0", "tadd2", "tz1", "tz2",
+    "near1", "head0", "head1", "head2", "head3", "near3", "down0", "head4",
+    "down1", "far1", "query0", "near0", "far3", "near2", "aend0", "tready0",
+    "far0", "fadd1", "down2", "fadd3", "tnear3", "tnear1", "down3", "down4",
+    "far2", "fadd0", "down5", "fz0", "tnear0", "tnear2", "fadd2", "dfirst0",
+    "tfar3", "fz1", "tfar0", "tfar2", "fz2", "tfar1", "tadd0", "dsecond0",
+    "ftotal0", "tadd2", "tadd3", "dgather0", "tz0", "tz1", "tadd1", "tz2",
     "fmiddle0", "ttotal0", "dmiddle0",
 )
 END_ORDER = (
-    "near1", "head0", "near0", "down0", "far1", "head1", "down1", "down2",
-    "head2", "head3", "head4", "near3", "down3", "far0", "fadd1", "down4",
-    "query0", "near2", "aend0", "down5", "fadd0", "far3", "fz0", "tready0",
-    "tnear3", "far2", "fadd3", "tnear0", "fz2", "tnear2", "fadd2", "fz1",
-    "tnear1", "tfar3", "tfar0", "dfirst0", "tfar2", "tfar1", "tadd0", "tadd3",
-    "tz0", "tadd1", "dsecond0", "tz2", "ftotal0", "tadd2", "tz1", "dgather0",
-    "ttotal0", "fmiddle0", "dmiddle0",
+    "near0", "down0", "head0", "head1", "down1", "near1", "head2", "head3",
+    "head4", "far0", "near3", "down2", "query0", "far1", "down3", "down4",
+    "near2", "aend0", "fadd0", "tready0", "down5", "fadd1", "fz0", "tnear3",
+    "far3", "far2", "tnear0", "fadd3", "fz2", "tnear2", "fadd2", "tnear1",
+    "fz1", "tfar3", "tfar0", "dfirst0", "tadd0", "tfar2", "tfar1", "tadd3",
+    "tz0", "dsecond0", "tadd1", "tz2", "ftotal0", "tadd2", "tz1", "dgather0",
+    "fmiddle0", "ttotal0", "dmiddle0",
 )
 
 
@@ -867,7 +877,7 @@
     def some(start, size, unit=16):
         return pl.ds(pl.multiple_of(start, unit), size)
 
-    gain_load = pltpu.make_async_copy(gain_h, gain_rows.at[pl.ds(0, gain_h.shape[0])], load.at[7])
+    gain_load = pltpu.make_async_copy(gain_h, gain_rows.at[pl.ds(0, gain_h.shape[0])], load.at[9])
     by_need = ((3, 2, 1, 0), (3, 0, 2, 1), (0, 3, 1, 2), (0, 1, 2, 3))
     by_turns = ((3, 2, 1, 0), (3, 0, 2, 1), (0, 3, 1, 2), (0, 2, 1, 3))
 
@@ -882,8 +892,16 @@
     loads = [None] + [
         pltpu.make_async_copy(h, v, load.at[1 + i])
         for i, (h, v) in enumerate(
-            [(br_h, br_v), (nf_h, stage), (gg_h, gg_v), (gu_h, gu_v), (la_h, stage), (nr_h, stage)]
-        )
+            [(br_h, br_v), (nf_h, stage), (la_h, stage), (nr_h, stage)]
+        )
+    ]
+    halves = [
+        [
+            pltpu.make_async_copy(h.at[:, span], v.at[:, span], load.at[slot + 2 * own])
+            for h, v, first, slot in ((gg_h, gg_v, x, 5), (gu_h, gu_v, y, 6))
+            for span in (some((own * first + (1 - own) * (1 - first)) * quarter, quarter, 128),)
+        ]
+        for own in range(2)
     ]
     kept = [
         pltpu.make_async_copy(h, v, kept_sem.at[i])
@@ -907,8 +925,8 @@
         for i, h in enumerate((wk_h, wv_h))
     ]
     loads[2].start()
-    loads[3].start()
-    loads[4].start()
+    for copy in halves[0]:
+        copy.start()
     gain_rows[...] = jnp.zeros_like(gain_rows)
 
     barrier = pltpu.get_barrier_semaphore()
@@ -1257,13 +1275,13 @@
         grads_out.start(go, 0)
 
     def t_ready():
-        loads[5].wait()
+        loads[3].wait()
         turn(stage, ln_t)
-        loads[6].start()
+        loads[4].start()
         block_of = lambda at, size: wide(gain_rows[:, at : at + size]).T
         for at, size in tiles(width, 128):
             gain_t[at : at + size, :] = pltpu.roll(block_of(at, size), 64, 1)[:size]
-        loads[6].wait()
+        loads[4].wait()
         turn(stage, ln_t, width)
         for copy in late:
             copy.wait()
@@ -1278,7 +1296,7 @@
     def head_step(g):
         @pl.when(g == 0)
         def _():
-            for copy in kept[:6]:
+            for copy in halves[1] + kept[:6]:
                 copy.wait()
             ra[1] = gm[...].astype(BF16)
 
@@ -1332,14 +1350,14 @@
 
     loads[2].wait()
     turn(stage, nf_t)
-    loads[3].wait()
-    loads[4].wait()
+    for copy in halves[0]:
+        copy.wait()
     in_load(0).start()
     loads[1].start()
-    for copy in kept + weights + late + [gain_load]:
+    for copy in halves[1] + kept + weights + late + [gain_load]:
         copy.start()
     pl.semaphore_wait(barrier, 7 + not_first + not_last)
-    loads[5].start()
+    loads[3].start()
 
     def one(n, carry):
         code = (1 - edge) * pick(n, tables[0]) + edge * pick(n, tables[1])
@@ -1447,7 +1465,7 @@
             b(RANKS, part, wide_t), b(RANKS, part, wide_t),
             b(RANKS, part // 2, wide_t), b(RANKS, part // 2, wide_t), b(RANKS, part // 2, wide_t), b(5, part // 2, wide_t),
             b(2, 2, 4, fine // 4, columns), b(2, 2, 4, part, quarter), b(2, 4, part // 2, wide_t),
-            sem(8), sem(7), sem(5, KEY_VALUE_HEADS), sem(2, KEY_VALUE_HEADS), sem(3, KEY_VALUE_HEADS), sem(2), sem(2), sem(2), sem(2), sem(2),
+            sem(10), sem(7), sem(5, KEY_VALUE_HEADS), sem(2, KEY_VALUE_HEADS), sem(3, KEY_VALUE_HEADS), sem(2), sem(2), sem(2), sem(2), sem(2),
             sem(3, 2), sem(5, 2), sem(2), sem(2), sem(2), sem(2),
             sem(2, 2), sem(2, 4), sem(2, 2), sem(2, 4), sem(2, 3), sem(2, 5),
             sem(4), sem(4), sem(4), sem(4), sem(3), sem(5),

time: 197 us -> 196 us (level)
  Pallas kernels: 196 us -> 194 us
    pallas_call x1, Pallas kernels: 71.9 us -> 69.4 us  [run_layers(): pl.pallas_call(lambda *refs: layers_kernel(complete, *refs), out_shape=[o...]
where the time goes in v2:
time: 196 us; the launch traced here: 194 us
  Pallas kernels  194 us (99%)
    pallas_call x1, Pallas kernels, run_sums(): pl.pallas_call(sums_kernel, out_shape=[out(*ends_shape), out(2, per, wide...  116 us
    pallas_call x1, Pallas kernels, run_layers(): pl.pallas_call(lambda *refs: layers_kernel(complete, *refs), out_shape=[o...  69.4 us
    pallas_call x1, Pallas kernels, run_finish(): pl.pallas_call(finish_kernel, out_shape=[jax.ShapeDtypeStruct(acts.shape,...  7.76 us

profile of v2, /device:TPU:0, one launch (start us, length us, event | category | flops | bytes accessed | tf_op | source)
XLA Modules:
  0.0 194.5 jit_solution(4656720858262926051)
XLA Ops:
  0.6 69.4 %layers.1 = (bf16[1,2,224,960]{3,2,1,0:T(8,128)(2,1)}, bf16[1,2,224,960]{3,2,1,0:T(8,128)(2,1)}, f32[8,960]{1,0:T(8,128)}, bf16[896,960]{1,0:T(8,128)(2,1)}, bf1...) custom-call(s32[2,1,2]{2,1,0:T(1,128)} %refs_0_.1, ...), custom_call_target="tpu_custom_call" | custom-call | tf_op jit(solution)/shard_map/layers/pallas_call | solution.py:731
  70.0 116.5 %sums.1 = (bf16[1,2,224,960]{3,2,1,0:T(8,128)(2,1)}, bf16[2,240,1408]{2,1,0:T(8,128)(2,1)}, bf16[240,2560]{1,0:T(8,128)(2,1)}, bf16[240,2560]{1,0:T(8,128)(2,1)}, bf16[640,1024]{1,0:T(8,128)(2,1)}) custom-call(f32[8,960]{1,0:T(8,128)} %get-tuple-element.47.refs_0_, bf16[960]{0:T(1024)(128)(2,1)} %refs_1_.3, bf16[896,960]{1,0:T(8,128)(2,1)} %get-tuple-element.48.refs_2_, ...), custom_call_target="tpu_custom_call" | custom-call | tf_op jit(solution)/shard_map/sums/pallas_call | solution.py:1446
  186.5 7.8 %finish.1 = (bf16[1,2,224,960]{3,2,1,0:T(8,128)(2,1)}, bf16[1,2,224,960]{3,2,1,0:T(8,128)(2,1)}, f32[240,960]{1,0:T(8,128)}, f32[240,960]{1,0:T(8,128)}, f32[320...) custom-call(bf16[1,2,224,960]{3,2,1,0:T(8,128)(2,1)} %get-tuple-elem, ...), custom_call_target="tpu_custom_call" | custom-call | tf_op jit(solution)/shard_map/finish/pallas_call | solution.py:1549

commit v3 on v2

--- a/solution.py
+++ b/solution.py
@@ -1509,10 +1509,6 @@
         loads[k].wait()
         gate_f[k] = gate_v[k].astype(F32)
         stores[2 + k].start()
-    loads[4].wait()
-    stores[0].start()
-    pltpu.make_async_copy(first_h, row_v.at[1], load.at[5]).wait()
-    stores[1].start()
     loads[2].wait()
     for at, size in tiles(width, 128):
         down_f[at : at + size, :] = down_v[:, at : at + 128].astype(F32).T[:size]
@@ -1537,6 +1533,10 @@
     gain_rows = both.T
     gain_a[...] = gain_rows[row]
     gain_f[...] = gain_rows[row + 1]
+    loads[4].wait()
+    stores[0].start()
+    pltpu.make_async_copy(first_h, row_v.at[1], load.at[5]).wait()
+    stores[1].start()
     for copy in stores:
         copy.wait()
 

time: 196 us -> 194 us (0.990)
  Pallas kernels: 194 us -> 192 us
where the time goes in v3:
time: 194 us; the launch traced here: 193 us
  Pallas kernels  192 us (99%)
    pallas_call x1, Pallas kernels, run_sums(): pl.pallas_call(sums_kernel, out_shape=[out(*ends_shape), out(2, per, wide...  116 us
    pallas_call x1, Pallas kernels, run_layers(): pl.pallas_call(lambda *refs: layers_kernel(complete, *refs), out_shape=[o...  69.4 us
    pallas_call x1, Pallas kernels, run_finish(): pl.pallas_call(finish_kernel, out_shape=[jax.ShapeDtypeStruct(acts.shape,...  6.61 us

profile of v3, /device:TPU:0, one launch (start us, length us, event | category | flops | bytes accessed | tf_op | source)
XLA Modules:
  0.0 193.3 jit_solution(13685217771304626930)
XLA Ops:
  0.6 69.4 %layers.1 = (bf16[1,2,224,960]{3,2,1,0:T(8,128)(2,1)}, bf16[1,2,224,960]{3,2,1,0:T(8,128)(2,1)}, f32[8,960]{1,0:T(8,128)}, bf16[896,960]{1,0:T(8,128)(2,1)}, bf1...) custom-call(s32[2,1,2]{2,1,0:T(1,128)} %refs_0_.1, ...), custom_call_target="tpu_custom_call" | custom-call | tf_op jit(solution)/shard_map/layers/pallas_call | solution.py:731
  70.0 116.5 %sums.1 = (bf16[1,2,224,960]{3,2,1,0:T(8,128)(2,1)}, bf16[2,240,1408]{2,1,0:T(8,128)(2,1)}, bf16[240,2560]{1,0:T(8,128)(2,1)}, bf16[240,2560]{1,0:T(8,128)(2,1)}, bf16[640,1024]{1,0:T(8,128)(2,1)}) custom-call(f32[8,960]{1,0:T(8,128)} %get-tuple-element.47.refs_0_, bf16[960]{0:T(1024)(128)(2,1)} %refs_1_.3, bf16[896,960]{1,0:T(8,128)(2,1)} %get-tuple-element.48.refs_2_, ...), custom_call_target="tpu_custom_call" | custom-call | tf_op jit(solution)/shard_map/sums/pallas_call | solution.py:1446
  186.5 6.6 %finish.1 = (bf16[1,2,224,960]{3,2,1,0:T(8,128)(2,1)}, bf16[1,2,224,960]{3,2,1,0:T(8,128)(2,1)}, f32[240,960]{1,0:T(8,128)}, f32[240,960]{1,0:T(8,128)}, f32[320...) custom-call(bf16[1,2,224,960]{3,2,1,0:T(8,128)(2,1)} %get-tuple-elem, ...), custom_call_target="tpu_custom_call" | custom-call | tf_op jit(solution)/shard_map/finish/pallas_call | solution.py:1549

commit v4 on v3

--- a/solution.py
+++ b/solution.py
@@ -1498,17 +1498,18 @@
         )
     ]
     section = lax.axis_index("section")
-    for copy in loads:
+    for copy in loads[:4]:
         copy.start()
+    for k in range(2):
+        loads[k].wait()
+        gate_f[k] = gate_v[k].astype(F32)
+        stores[2 + k].start()
+    loads[4].start()
     start_if(
         section == 0,
         lambda: pltpu.make_async_copy(first_h, row_v.at[1], load.at[5]),
         lambda: pltpu.make_async_copy(second_h, row_v.at[1], load.at[5]),
     )
-    for k in range(2):
-        loads[k].wait()
-        gate_f[k] = gate_v[k].astype(F32)
-        stores[2 + k].start()
     loads[2].wait()
     for at, size in tiles(width, 128):
         down_f[at : at + size, :] = down_v[:, at : at + 128].astype(F32).T[:size]

time: 194 us -> 195 us (level)
  no operation moved by 1% of the time
where the time goes in v4:
time: 195 us; the launch traced here: 193 us
  Pallas kernels  192 us (98%)
    pallas_call x1, Pallas kernels, run_sums(): pl.pallas_call(sums_kernel, out_shape=[out(*ends_shape), out(2, per, wide...  116 us
    pallas_call x1, Pallas kernels, run_layers(): pl.pallas_call(lambda *refs: layers_kernel(complete, *refs), out_shape=[o...  69.4 us
    pallas_call x1, Pallas kernels, run_finish(): pl.pallas_call(finish_kernel, out_shape=[jax.ShapeDtypeStruct(acts.shape,...  6.64 us

profile of v4, /device:TPU:0, one launch (start us, length us, event | category | flops | bytes accessed | tf_op | source)
XLA Modules:
  0.0 193.3 jit_solution(9296687124338116631)
XLA Ops:
  0.6 69.4 %layers.1 = (bf16[1,2,224,960]{3,2,1,0:T(8,128)(2,1)}, bf16[1,2,224,960]{3,2,1,0:T(8,128)(2,1)}, f32[8,960]{1,0:T(8,128)}, bf16[896,960]{1,0:T(8,128)(2,1)}, bf1...) custom-call(s32[2,1,2]{2,1,0:T(1,128)} %refs_0_.1, ...), custom_call_target="tpu_custom_call" | custom-call | tf_op jit(solution)/shard_map/layers/pallas_call | solution.py:731
  70.0 116.5 %sums.1 = (bf16[1,2,224,960]{3,2,1,0:T(8,128)(2,1)}, bf16[2,240,1408]{2,1,0:T(8,128)(2,1)}, bf16[240,2560]{1,0:T(8,128)(2,1)}, bf16[240,2560]{1,0:T(8,128)(2,1)}, bf16[640,1024]{1,0:T(8,128)(2,1)}) custom-call(f32[8,960]{1,0:T(8,128)} %get-tuple-element.47.refs_0_, bf16[960]{0:T(1024)(128)(2,1)} %refs_1_.3, bf16[896,960]{1,0:T(8,128)(2,1)} %get-tuple-element.48.refs_2_, ...), custom_call_target="tpu_custom_call" | custom-call | tf_op jit(solution)/shard_map/sums/pallas_call | solution.py:1446
  186.5 6.6 %finish.1 = (bf16[1,2,224,960]{3,2,1,0:T(8,128)(2,1)}, bf16[1,2,224,960]{3,2,1,0:T(8,128)(2,1)}, f32[240,960]{1,0:T(8,128)}, f32[240,960]{1,0:T(8,128)}, f32[320...) custom-call(bf16[1,2,224,960]{3,2,1,0:T(8,128)(2,1)} %get-tuple-elem, ...), custom_call_target="tpu_custom_call" | custom-call | tf_op jit(solution)/shard_map/finish/pallas_call | solution.py:1550
